TPU v7x, 512 devices: a whole 4x4x16 slice. The times are simulated.
512 devices in a mesh: rows: 32 (over z, core), cols: 16 (over x, y).
Axes of the slice: x: 4, y: 4, z: 16, core: 2. Of those that a mesh axis runs over, the one named last changes fastest.
Arguments:
- tile_values: bfloat16 [16384, 256, 256], P(('rows', 'cols')), may hold values from 0 to 30, as said below
- tile_rows: int32 [16384], P(('rows', 'cols')), may hold values from 0 to 15, as said below
- tile_cols: int32 [16384], P(('rows', 'cols')), may hold values from 0 to 31, as said below
- live_count: int32 [512], P(('rows', 'cols')), may hold values from 16 to 32, as said below
- initial: bfloat16 [131072, 128], P(('rows', 'cols')), may hold values from -6 to 6
Outputs:
- basis: float32 [131072, 128], P(('rows', 'cols'))
Inputs may be any that keep to these rules, and one draw needn't show every extreme that they name: `tile_values`: every row and every column of each tile holds a positive entry. `tile_rows`: on every device the first 16 slots name each of its block rows once; further slots favour low block rows. `tile_cols`: slot 0 of the device at rows index r names block column r. `live_count`: some device has all 32 slots live.
All inputs are finite; a program needn't handle non-finite values.
Results may differ from a plain program's by a relative error of at most 0.02.
Values may be sent and summed in bfloat16 or wider, within the bound.
No kernel may reach another device: no remote copies, remote signals or barrier semaphores. Data moves between devices by JAX's collectives and lax.ppermute only.
A program may use at most 64 MiB of HBM per device.

v0:
```python
import jax
import jax.numpy as jnp
from jax import lax
from jax.sharding import PartitionSpec as P

ITERS = 2


def shards(tile_values, tile_rows, tile_cols, live_count, initial):
    row_count = lax.axis_size("rows")
    col_count = lax.axis_size("cols")
    slot_count = tile_values.shape[0]
    tile_side = tile_values.shape[1]
    width = initial.shape[1]
    highest = lax.Precision.HIGHEST
    positions = jnp.arange(slot_count, dtype=jnp.int32)
    live_mask = (positions < live_count[0]).astype(jnp.float32)
    row_pick = (jnp.arange(col_count, dtype=jnp.int32)[:, None] == tile_rows[None, :]).astype(
        jnp.float32
    ) * live_mask[None, :]
    col_pick = (jnp.arange(row_count, dtype=jnp.int32)[:, None] == tile_cols[None, :]).astype(
        jnp.float32
    ) * live_mask[None, :]
    row_sums = jnp.sum(tile_values, axis=2, dtype=jnp.float32)
    col_sums = jnp.sum(tile_values, axis=1, dtype=jnp.float32)
    row_part = jnp.dot(row_pick, row_sums, precision=highest, preferred_element_type=jnp.float32)
    own_degree = lax.psum_scatter(
        row_part.reshape(col_count * tile_side), "cols", scatter_dimension=0, tiled=True
    )
    col_part = jnp.dot(col_pick, col_sums, precision=highest, preferred_element_type=jnp.float32)
    col_degree = lax.psum(col_part, "rows")
    row_scale = lax.rsqrt(own_degree)[:, None]
    col_scale = lax.rsqrt(col_degree)[:, :, None]
    current = initial
    fresh = jnp.zeros((tile_side, width), jnp.float32)
    lower = jnp.eye(width, dtype=jnp.float32)
    basis = fresh
    for sweep in range(ITERS):
        arrived = lax.all_gather(current, "rows", axis=0, tiled=True)
        scaled = (
            col_scale * arrived.reshape(row_count, tile_side, width).astype(jnp.float32)
        ).astype(jnp.bfloat16)
        product = jnp.einsum(
            "stu,suk->stk", tile_values, scaled[tile_cols], preferred_element_type=jnp.float32
        )
        partial_value = jnp.einsum(
            "bs,stk->btk", row_pick, product, precision=highest, preferred_element_type=jnp.float32
        )
        flat_partial = partial_value.reshape(col_count * tile_side, width)
        summed = lax.psum_scatter(
            flat_partial.astype(jnp.bfloat16), "cols", scatter_dimension=0, tiled=True
        ).astype(jnp.float32)
        fresh = row_scale * summed
        gram = jnp.dot(fresh.T, fresh, precision=highest, preferred_element_type=jnp.float32)
        gram = lax.psum(gram, ("rows", "cols"))
        lower = jnp.linalg.cholesky(gram)
        basis = lax.linalg.triangular_solve(
            lower, fresh, left_side=False, lower=True, transpose_a=True
        )
        current = basis.astype(jnp.bfloat16)
    return basis


def solution(mesh):
    in_specs = (
        P(("rows", "cols"), None, None),
        P(("rows", "cols")),
        P(("rows", "cols")),
        P(("rows", "cols")),
        P(("rows", "cols"), None),
    )
    out_specs = P(("rows", "cols"), None)
    return jax.shard_map(shards, mesh=mesh, in_specs=in_specs, out_specs=out_specs, check_vma=False)
```

profile of v0, /device:TPU:1, one launch (start us, length us, event | category | flops | bytes accessed | tf_op | source)
XLA Modules:
  0.0 1348.1 jit_solution(16155573127566439082)
XLA Ops:
  8.0 3.8 convert_reduce_fusion.1
  11.9 97.9 %psum.21 = f32[32,256]{1,0:T(8,128)S(1)} all-reduce(f32[32,256]{1,0:T(8,128)S(1)} %fusion.16), channel_id=1, replica_groups=mesh['rows'=32,'cols'=16] {'rows'}, use_global_device_ids=true, to_apply=%region_3.0 | all-reduce | flops 8192 | bytes 65536 | tf_op jit(solution)/shard_map/psum | solution.py:31
  109.9 3.4 fusion
  113.3 2.5 gather_fusion
  115.9 5.6 convolution_bitcast_fusion.1
  121.5 5.5 copy.21
  127.0 4.3 convolution_convert_fusion.1
  131.3 1.3 copy.22
  132.8 1.3 dynamic-slice
  134.7 61.6 %all-reduce = f32[4096]{0:T(1024)S(1)} all-reduce(f32[4096]{0:T(1024)S(1)} %bitcast.55), channel_id=2, replica_groups=mesh['rows'=32,'cols'=16] {'cols'}, use_global_device_ids=true, to_apply=%region_1.0.clone | all-reduce | flops 4096 | bytes 32768
  196.4 22.1 %reduce-scatter.3.cloned.1.call-done = bf16[256,128]{1,0:T(8,128)(2,1)} async-done(((bf16[4096,128]{1,0:T(8,128)(2,1)}), bf16[256,128]{1,0:T(8,128)(2,1)}) %reduce-scatter.3.cloned.1.call-update) | async-done | bytes 65552 | tf_op jit(solution)/shard_map/reduce_scatter | solution.py:50
  218.5 2.0 fusion.3
  220.8 445.6 %all-reduce.4.cloned.1.call-done = f32[128,128]{0,1:T(8,128)} async-done(((f32[128,128]{0,1:T(8,128)}), f32[128,128]{0,1:T(8,128)}) %all-reduce.4.cloned.1.call-update) | async-done | bytes 65552 | tf_op jit(solution)/shard_map/psum | solution.py:55
  666.4 0.9 copy.24
  668.2 11.7 cholesky.44
  681.2 9.8 custom-call.6
  691.0 1.8 fusion.1
  693.0 65.2 %all-gather.5.cloned.1.call-done = bf16[8192,128]{0,1:T(8,128)(2,1)} async-done(((bf16[256,128]{0,1:T(8,128)(2,1)}), bf16[8192,128]{0,1:T(8,128)(2,1)}) %all-gather.5.cloned.1.call-update) | async-done | bytes 2097168 | tf_op jit(solution)/shard_map/all_gather | solution.py:39
  758.1 4.3 copy.36
  762.4 2.8 multiply_convert_fusion
  765.3 2.1 gather_fusion.1
  767.4 6.3 convolution_bitcast_fusion
  773.7 5.5 copy.27
  779.2 4.3 convolution_convert_fusion
  783.5 1.3 copy.28
  785.0 82.0 %reduce-scatter.5.cloned.1.call-done = bf16[256,128]{1,0:T(8,128)(2,1)} async-done(((bf16[4096,128]{1,0:T(8,128)(2,1)}), bf16[256,128]{1,0:T(8,128)(2,1)}) %reduce-scatter.5.cloned.1.call-update) | async-done | bytes 65552 | tf_op jit(solution)/shard_map/reduce_scatter | solution.py:50
  867.0 2.0 fusion.2
  869.0 445.6 %all-reduce.6.cloned.1.call-done = f32[128,128]{0,1:T(8,128)} async-done(((f32[128,128]{0,1:T(8,128)}), f32[128,128]{0,1:T(8,128)}) %all-reduce.6.cloned.1.call-update) | async-done | bytes 65552 | tf_op jit(solution)/shard_map/psum | solution.py:55
  1314.6 0.9 copy.30
  1316.4 11.7 cholesky.55
  1329.5 9.8 custom-call.7
  1339.3 1.2 convolution_bitcast_fusion.2
  (34 shorter events, 7.0 us)
Async XLA Ops:
  6.5 5.2 copy-start.1
  6.5 103.3 %all-gather.3.cloned.1.call-start = ((), (), s32[]{:S(2)}) async-start(), calls=%async_computation.2 | async-start | bytes 2162688 | tf_op jit(solution)/shard_map/all_gather | solution.py:39
  7.3 211.2 %reduce-scatter.3.cloned.1.call-start = ((), (), s32[]{:S(2)}) async-start(), calls=%async_computation.3 | async-start | bytes 1114112 | tf_op jit(solution)/shard_map/reduce_scatter | solution.py:50
  121.5 5.5 copy-start
  132.6 533.8 %all-reduce.4.cloned.1.call-start = ((), (), s32[]{:S(2)}) async-start(), calls=%async_computation.4 | async-start | bytes 131072 | tf_op jit(solution)/shard_map/psum | solution.py:55
  220.5 537.6 %all-gather.5.cloned.1.call-start = ((), (), s32[]{:S(2)}) async-start(), calls=%async_computation.5 | async-start | bytes 2162688 | tf_op jit(solution)/shard_map/all_gather | solution.py:39
  692.9 174.1 %reduce-scatter.5.cloned.1.call-start = ((), (), s32[]{:S(2)}) async-start(), calls=%async_computation.6 | async-start | bytes 1114112 | tf_op jit(solution)/shard_map/reduce_scatter | solution.py:50
  784.7 529.9 %all-reduce.6.cloned.1.call-start = ((), (), s32[]{:S(2)}) async-start(), calls=%async_computation.7 | async-start | bytes 131072 | tf_op jit(solution)/shard_map/psum | solution.py:55
Sparse Core Ops, SparseCore 0:
  9.5 77.5 all-gather.2
  132.7 85.7 reduce-scatter.2
  224.8 441.5 all-reduce.3
  693.0 65.0 all-gather.4
  784.9 82.0 reduce-scatter.4
  873.2 441.4 all-reduce.5
where the time goes:
time: 1350 us
  waiting for transfers between devices  1060 us (79%)
  blocking collectives  160 us (12%)
  other arithmetic  57.5 us (4%)
  matrix products  27.8 us (2%)
  local copies, waits for them, and re-layouts  26.5 us (2%)
  between operations  14.9 us (1%)
    psum x2, waiting for transfers between devices, shards(): gram = lax.psum(gram, ('rows', 'cols'))  891 us
    reduce_scatter x2, waiting for transfers between devices, shards(): lax.psum_scatter(flat_partial.astype(jnp.bfloat16), 'cols', scatter_dimen...  104 us
    psum x1, blocking collectives, shards(): col_degree = lax.psum(col_part, 'rows')  97.9 us
    all_gather x2, waiting for transfers between devices, shards(): arrived = lax.all_gather(current, 'rows', axis=0, tiled=True)  65.2 us
    unnamed x1, blocking collectives  61.6 us
  transfers between devices with their start and end apart: 6, of which 5 were waited for; matrix products, arithmetic and copies ran while one was open for 0% of the time, Pallas kernels for 0%

commit v1 on v0

v1 whole, which is shorter than its diff:
```python
import functools

import jax
import jax.numpy as jnp
import numpy as np
from jax import lax
from jax.experimental import pallas as pl
from jax.experimental.pallas import tpu as pltpu
from jax.sharding import Mesh, PartitionSpec as P

ZS = 16
PEERS = 16
SIDE = 256
WIDTH = 128
FIRST = 16
EXTRA = 32
VMEM_BYTES = 48 * 1024 * 1024
F32 = jnp.float32
BF16 = jnp.bfloat16
HIGHEST = lax.Precision.HIGHEST

params = pltpu.CompilerParams(vmem_limit_bytes=VMEM_BYTES)
smem = pl.BlockSpec(memory_space=pltpu.SMEM)
vmem = pl.BlockSpec(memory_space=pltpu.VMEM)


def eye_mask():
    return lax.broadcasted_iota(jnp.int32, (WIDTH, WIDTH), 0) == lax.broadcasted_iota(
        jnp.int32, (WIDTH, WIDTH), 1
    )


def to_column(lanes):
    spread = jnp.broadcast_to(lanes, (WIDTH, WIDTH))
    return jnp.sum(jnp.where(eye_mask(), spread, 0.0), axis=1, keepdims=True)


def split3(value):
    high = value.astype(BF16)
    rest = value - high.astype(F32)
    middle = rest.astype(BF16)
    low = (rest - middle.astype(F32)).astype(BF16)
    return high, middle, low


def degree_kernel(cols_ref, live_ref, tiles_ref, out_ref, acc_ref):
    acc_ref[...] = jnp.zeros_like(acc_ref)

    def one(slot, carry):
        tile = tiles_ref[slot].astype(F32).reshape(SIDE // 8, 8, SIDE)
        acc_ref[cols_ref[slot]] += jnp.sum(tile, axis=0)
        return carry

    lax.fori_loop(0, live_ref[0], one, 0)
    out_ref[...] = jnp.zeros_like(out_ref)
    for block in range(2 * ZS):
        total = jnp.sum(acc_ref[block], axis=0, keepdims=True)
        at = 2 * (block % 2)
        out_ref[block // 2, at : at + 1, :] = total[:, :WIDTH]
        out_ref[block // 2, at + 1 : at + 2, :] = total[:, WIDTH:]


def scale_kernel(mine_ref, other_ref, initial_ref, out_ref, scale_ref):
    degree = mine_ref[...] + other_ref[...]
    scale = lax.rsqrt(degree)
    scale_ref[...] = scale
    for half in range(2):
        rows = slice(half * WIDTH, (half + 1) * WIDTH)
        column = to_column(scale[half : half + 1])
        scaled = (column * initial_ref[rows].astype(F32)).astype(BF16)
        for peer in range(ZS):
            out_ref[peer, rows] = scaled


def product_kernel(with_rows, core_ref, rows_ref, cols_ref, live_ref, tiles_ref, mine_ref, other_ref, out_ref, acc_ref):
    core = core_ref[0]

    def product(slot):
        col = cols_ref[slot]
        at = lax.div(col, 2)
        same = lax.rem(col, 2) == core
        block = jnp.where(same, mine_ref[at, :SIDE], other_ref[at, :SIDE])
        if with_rows:
            block = jnp.concatenate([block, jnp.ones((SIDE, WIDTH), BF16)], axis=1)
        return jnp.dot(tiles_ref[slot], block, preferred_element_type=F32)

    def first(slot, carry):
        acc_ref[rows_ref[slot]] = product(slot)
        return carry

    def later(slot, carry):
        acc_ref[rows_ref[slot]] += product(slot)
        return carry

    lax.fori_loop(0, FIRST, first, 0, unroll=4)
    lax.fori_loop(FIRST, live_ref[0], later, 0)
    if with_rows:
        eye = eye_mask()
        zero = jnp.zeros((EXTRA - 6, WIDTH), BF16)
        for block in range(PEERS):
            out_ref[block, :SIDE] = acc_ref[block, :, :WIDTH].astype(BF16)
            pieces = []
            for half in range(2):
                spread = acc_ref[block, half * WIDTH : (half + 1) * WIDTH, WIDTH:]
                pieces.append(jnp.sum(jnp.where(eye, spread, 0.0), axis=0, keepdims=True))
            parts = split3(jnp.concatenate(pieces, axis=0))
            out_ref[block, SIDE:] = jnp.concatenate(list(parts) + [zero], axis=0)
    else:
        gram = jnp.zeros((8, WIDTH), F32)
        for at in range(ZS):
            for ref in (mine_ref, other_ref):
                extra = ref[at, SIDE:].astype(F32)
                gram += extra[0:8] + extra[8:16] + extra[16:24]
        extra = jnp.concatenate(list(split3(gram)) + [jnp.zeros((8, WIDTH), BF16)], axis=0)
        for block in range(PEERS):
            out_ref[block, :SIDE] = acc_ref[block].astype(BF16)
            out_ref[block, SIDE:] = extra


def total_of(ref, rows):
    total = ref[0, rows].astype(F32)
    for peer in range(1, PEERS):
        total += ref[peer, rows].astype(F32)
    return total


def gram_of(fresh):
    return lax.dot_general(
        fresh, fresh, (((0,), (0,)), ((), ())), precision=HIGHEST, preferred_element_type=F32
    )


def middle_kernel(arrived_ref, col_scale_ref, out_ref, row_scale_ref):
    extra = total_of(arrived_ref, slice(SIDE, SIDE + EXTRA))
    degree = extra[0:2] + extra[2:4] + extra[4:6]
    row_scale = lax.rsqrt(degree)
    row_scale_ref[...] = row_scale
    halves = []
    for half in range(2):
        rows = slice(half * WIDTH, (half + 1) * WIDTH)
        fresh = to_column(row_scale[half : half + 1]) * total_of(arrived_ref, rows)
        halves.append(fresh)
        scaled = (to_column(col_scale_ref[half : half + 1]) * fresh).astype(BF16)
        for peer in range(ZS):
            out_ref[peer, rows] = scaled
    gram = gram_of(jnp.concatenate(halves, axis=0))
    zero = jnp.zeros((8, WIDTH), BF16)
    for peer in range(ZS):
        piece = gram[8 * peer : 8 * peer + 8]
        out_ref[peer, SIDE:] = jnp.concatenate(list(split3(piece)) + [zero], axis=0)


def last_kernel(arrived_ref, row_scale_ref, fresh_ref, gram_ref, first_gram_ref):
    halves = []
    for half in range(2):
        rows = slice(half * WIDTH, (half + 1) * WIDTH)
        fresh = to_column(row_scale_ref[half : half + 1]) * total_of(arrived_ref, rows)
        fresh_ref[rows] = fresh
        halves.append(fresh)
    gram_ref[...] = gram_of(jnp.concatenate(halves, axis=0))
    extra = total_of(arrived_ref, slice(SIDE, SIDE + EXTRA))
    first_gram_ref[...] = extra[0:8] + extra[8:16] + extra[16:24]


def lower_inverse(matrix):
    groups = WIDTH // 8
    parts = [matrix[8 * g : 8 * g + 8] for g in range(groups)]
    lane = lax.broadcasted_iota(jnp.int32, (8, WIDTH), 1)
    row = lax.broadcasted_iota(jnp.int32, (8, WIDTH), 0)
    roots = [jnp.zeros((8, WIDTH), F32) for _ in range(groups)]
    for k in range(WIDTH):
        g, r = divmod(k, 8)
        pivot_row = jnp.broadcast_to(parts[g][r : r + 1], (8, WIDTH))
        pivot = jnp.broadcast_to(parts[g][r : r + 1, k : k + 1], (8, WIDTH))
        roots[g] = jnp.where(row == r, pivot, roots[g])
        inverse = 1.0 / pivot
        at_k = lane == k
        source = jnp.where(at_k, 1.0, pivot_row) * inverse
        for h in range(g, groups):
            factor = jnp.broadcast_to(parts[h][:, k : k + 1], (8, WIDTH))
            kept = jnp.where(at_k, 0.0, parts[h])
            changed = kept - factor * source
            if h == g:
                parts[h] = jnp.where(row > r, changed, parts[h])
            else:
                parts[h] = changed
    out = []
    for g in range(groups):
        below = lane < row + 8 * g
        unit = jnp.where(below, parts[g], jnp.where(lane == row + 8 * g, 1.0, 0.0))
        out.append(unit * lax.rsqrt(roots[g]))
    return jnp.concatenate(out, axis=0)


def dot(a, b, dims):
    return lax.dot_general(a, b, (dims, ((), ())), precision=HIGHEST, preferred_element_type=F32)


def finish_kernel(first_gram_ref, gram_ref, fresh_ref, out_ref):
    first = lower_inverse(first_gram_ref[...])
    gram = dot(dot(first, gram_ref[...], ((1,), (0,))), first, ((1,), (1,)))
    second = lower_inverse(gram)
    fresh = dot(fresh_ref[...], first, ((1,), (1,)))
    out_ref[...] = dot(fresh, second, ((1,), (1,)))


def shape(dims, dtype):
    return jax.ShapeDtypeStruct(dims, dtype)


def shards(tile_values, tile_rows, tile_cols, live_count, initial):
    core = lax.axis_index("core")
    core_at = jnp.full((1,), core, jnp.int32)
    swap = [(0, 1), (1, 0)]

    with jax.named_scope("col_degree"):
        part = pl.pallas_call(
            degree_kernel,
            out_shape=shape((ZS, 8, WIDTH), F32),
            in_specs=[smem, smem, vmem],
            out_specs=vmem,
            scratch_shapes=[pltpu.VMEM((2 * ZS, 8, SIDE), F32)],
            compiler_params=params,
        )(tile_cols, live_count, tile_values)
        pieces = jnp.sum(lax.all_to_all(part, "z", 0, 0, tiled=True), axis=0)
        mine = lax.dynamic_slice_in_dim(pieces, 2 * core, 2, 0)
        other = lax.ppermute(lax.dynamic_slice_in_dim(pieces, 2 - 2 * core, 2, 0), "core", swap)
    with jax.named_scope("scale"):
        sent, col_scale = pl.pallas_call(
            scale_kernel,
            out_shape=(shape((ZS, SIDE, WIDTH), BF16), shape((2, WIDTH), F32)),
            in_specs=[vmem] * 3,
            out_specs=(vmem, vmem),
            compiler_params=params,
        )(mine, other, initial)

    def gather(sent):
        mine = lax.all_to_all(sent, "z", 0, 0, tiled=True)
        return mine, lax.ppermute(mine, "core", swap)

    def product(with_rows, mine, other):
        return pl.pallas_call(
            functools.partial(product_kernel, with_rows),
            out_shape=shape((PEERS, SIDE + EXTRA, WIDTH), BF16),
            in_specs=[smem] * 4 + [vmem] * 3,
            out_specs=vmem,
            scratch_shapes=[pltpu.VMEM((PEERS, SIDE, 2 * WIDTH if with_rows else WIDTH), F32)],
            compiler_params=params,
        )(core_at, tile_rows, tile_cols, live_count, tile_values, mine, other)

    with jax.named_scope("gather_one"):
        mine, other = gather(sent)
    with jax.named_scope("product_one"):
        partial_value = product(True, mine, other)
    with jax.named_scope("reduce_one"):
        arrived = lax.all_to_all(partial_value, ("x", "y"), 0, 0, tiled=True)
    with jax.named_scope("middle"):
        sent, row_scale = pl.pallas_call(
            middle_kernel,
            out_shape=(shape((ZS, SIDE + EXTRA, WIDTH), BF16), shape((2, WIDTH), F32)),
            in_specs=[vmem] * 2,
            out_specs=(vmem, vmem),
            compiler_params=params,
        )(arrived, col_scale)
    with jax.named_scope("gather_two"):
        mine, other = gather(sent)
    with jax.named_scope("product_two"):
        partial_value = product(False, mine, other)
    with jax.named_scope("reduce_two"):
        arrived = lax.all_to_all(partial_value, ("x", "y"), 0, 0, tiled=True)
    with jax.named_scope("last"):
        fresh, gram_part, first_piece = pl.pallas_call(
            last_kernel,
            out_shape=(shape((SIDE, WIDTH), F32), shape((WIDTH, WIDTH), F32), shape((8, WIDTH), F32)),
            in_specs=[vmem] * 2,
            out_specs=(vmem,) * 3,
            compiler_params=params,
        )(arrived, row_scale)
    with jax.named_scope("gram"):
        plane = ("core", "x", "y")
        count = 2 * PEERS
        deep = WIDTH // count
        piece = jnp.sum(
            lax.all_to_all(gram_part.reshape(count, deep, WIDTH), plane, 0, 0, tiled=True), axis=0
        )
        both = jnp.concatenate([first_piece, piece], axis=0)
        spread = jnp.broadcast_to(both[None], (ZS, 8 + deep, WIDTH))
        arrived = lax.all_to_all(spread, "z", 0, 0, tiled=True)
        first_gram = arrived[:, :8].reshape(WIDTH, WIDTH)
        piece = jnp.sum(arrived[:, 8:], axis=0)
        spread = jnp.broadcast_to(piece[None], (count, deep, WIDTH))
        gram = lax.all_to_all(spread, plane, 0, 0, tiled=True).reshape(WIDTH, WIDTH)
    with jax.named_scope("finish"):
        return pl.pallas_call(
            finish_kernel,
            out_shape=shape((SIDE, WIDTH), F32),
            in_specs=[vmem] * 3,
            out_specs=vmem,
            compiler_params=params,
        )(first_gram, gram, fresh)


def solution(mesh):
    devices = np.asarray(mesh.devices).reshape(ZS, 2, 4, 4)
    fine = Mesh(devices, ("z", "core", "x", "y"))
    whole = ("z", "core", "x", "y")
    in_specs = (P(whole, None, None), P(whole), P(whole), P(whole), P(whole, None))
    return jax.shard_map(
        shards, mesh=fine, in_specs=in_specs, out_specs=P(whole, None), check_vma=False
    )
```

time: 1350 us -> 305 us (0.23)
  waiting for transfers between devices: 1060 us -> 24.2 us
  other arithmetic: 57.5 us -> 0.09 us
  Pallas kernels: 0 us -> 46.1 us
  starting transfers between devices: 0.61 us -> 42.5 us
  matrix products: 27.8 us -> 0 us
  blocking collectives: 160 us -> 187 us
  local copies, waits for them, and re-layouts: 26.5 us -> 3.52 us
  between operations: 14.9 us -> 0.76 us
    psum x2 -> x0, waiting for transfers between devices: 891 us -> none  [shards(): gram = lax.psum(gram, ('rows', 'cols'))]
    all_to_all x0 -> x6, blocking collectives: none -> 187 us  [the longest x2 109 us: gather(): mine = lax.all_to_all(sent, 'z', 0, 0, tiled=True)]
    reduce_scatter x2 -> x0, waiting for transfers between devices: 104 us -> none  [shards(): lax.psum_scatter(flat_partial.astype(jnp.bfloat16), 'cols', scatter_dimen...]
    psum x1 -> x0, blocking collectives: 97.9 us -> none  [shards(): col_degree = lax.psum(col_part, 'rows')]
    all_gather x2 -> x0, waiting for transfers between devices: 65.2 us -> none  [shards(): arrived = lax.all_gather(current, 'rows', axis=0, tiled=True)]
    unnamed x1 -> x0, blocking collectives: 61.6 us -> none
    pallas_call x0 -> x7, Pallas kernels: none -> 46.1 us  [the longest x1 35.8 us: shards(): pl.pallas_call(finish_kernel, out_shape=shape((SIDE, WIDTH), F32), in_spe...]
    another operation x10 -> x0, other arithmetic: 45.7 us -> none  [the longest x6 24.8 us: shards(): lower = jnp.linalg.cholesky(gram)]
  transfers between devices with their start and end apart: 6 -> 5, of which waited for: 5 -> 5; matrix products, arithmetic and copies ran while one was open for 0% -> 0% of each run, Pallas kernels for 0% -> 0%
where the time goes in v1:
time: 305 us
  blocking collectives  187 us (61%)
  Pallas kernels  46.1 us (15%)
  starting transfers between devices  42.5 us (14%)
  waiting for transfers between devices  24.2 us (8%)
  local copies, waits for them, and re-layouts  3.52 us (1%)
    all_to_all x2, blocking collectives, gather(): mine = lax.all_to_all(sent, 'z', 0, 0, tiled=True)  109 us
    all_to_all x2, blocking collectives, shards(): arrived = lax.all_to_all(partial_value, ('x', 'y'), 0, 0, tiled=True)  50.1 us
    pallas_call x1, Pallas kernels, shards(): pl.pallas_call(finish_kernel, out_shape=shape((SIDE, WIDTH), F32), in_spe...  35.8 us
    all_to_all x1, blocking collectives, shards(): arrived = lax.all_to_all(spread, 'z', 0, 0, tiled=True)  16.1 us
    all_to_all x1, starting transfers between devices, shards(): pieces = jnp.sum(lax.all_to_all(part, 'z', 0, 0, tiled=True), axis=0)  16 us
    ppermute x2, starting transfers between devices, gather(): return (mine, lax.ppermute(mine, 'core', swap))  15.2 us
    all_to_all x1, blocking collectives, shards(): lax.all_to_all(gram_part.reshape(count, deep, WIDTH), plane, 0, 0, tiled=...  11.9 us
    all_to_all x1, waiting for transfers between devices, shards(): pieces = jnp.sum(lax.all_to_all(part, 'z', 0, 0, tiled=True), axis=0)  11.6 us
  transfers between devices with their start and end apart: 5, of which 5 were waited for; matrix products, arithmetic and copies ran while one was open for 0% of the time, Pallas kernels for 0%

profile of v1, /device:TPU:1, one launch (start us, length us, event | category | flops | bytes accessed | tf_op | source)
XLA Modules:
  0.0 304.6 jit_solution(4503642602419803408)
XLA Ops:
  0.7 0.0 copy-start
  0.7 2.2 copy-done
  2.8 0.0 copy-start.2
  2.8 0.7 copy-done.2
  3.5 0.0 copy-start.1
  3.5 1.8 col_degree.1
  5.3 16.0 %all-to-all-start = ((f32[16,8,128]{2,1,0:T(8,128)}), f32[16,8,128]{2,1,0:T(8,128)S(1)}, u32[]{:S(2)}, u32[]{:S(2)}) async-start(f32[16,8,128]{2,1,0:T(8,128)} %col_degree.1), calls=%async_computation | async-start | bytes 131072 | tf_op jit(solution)/shard_map/col_degree/all_to_all | solution.py:225
  21.3 11.6 %all-to-all-done = f32[16,8,128]{2,1,0:T(8,128)S(1)} async-done(((f32[16,8,128]{2,1,0:T(8,128)}), f32[16,8,128]{2,1,0:T(8,128)S(1)}, u32[]{:S(2)}, u32[]{:S(2)}) %all-to-all-start) | async-done | bytes 65568 | tf_op jit(solution)/shard_map/col_degree/all_to_all | solution.py:225
  32.9 4.1 %collective-permute-start = (f32[2,128]{1,0:T(2,128)S(1)}, f32[2,128]{1,0:T(2,128)S(1)}, u32[]{:S(2)}, u32[]{:S(2)}) collective-permute-start(f32[2,128]{1,0:T(2,128)S(1)} %get-tuple-element.19), channel_id=1, source_target_pairs={{0,16},{16,0},{1,17},{17,1},{2,18},{18,2},{3,19},{19,3},{4,20},{20... | collective-permute-start | bytes 3080 | tf_op jit(solution)/shard_map/col_degree/ppermute | solution.py:227
  37.0 0.8 collective-permute-done.other_ref
  37.8 0.0 copy-done.1
  37.8 0.2 scale.1
  38.0 47.7 %all_to_all.40.mine_ref = bf16[16,256,128]{2,1,0:T(8,128)(2,1)S(1)} all-to-all(bf16[16,256,128]{2,1,0:T(8,128)(2,1)S(1)} %get-tuple-element.12), channel_id=1, replica_groups=mesh['z'=16,'core'=2,'x'=4,'y'=4] {'z'}, dimensions={0} | all-to-all | bytes 2097152 | tf_op jit(solution)/shard_map/gather_one/all_to_all | solution.py:238
  85.7 9.3 %collective-permute-start.1 = (bf16[16,256,128]{2,1,0:T(8,128)(2,1)S(1)}, bf16[16,256,128]{2,1,0:T(8,128)(2,1)S(1)}, u32[]{:S(2)}, u32[]{:S(2)}) collective-permute-start(bf16[16,256,128]{2,1,0:T(8,128)(2,1)S(1)} %all_to_all.40.mine_ref), channel_id=1, source_target_pairs={{0,16},{16,0},{1,17},{17,1},{2,18},{18,2},{3,19},{19,3},{4,20},{20... | collective-permute-start | bytes 3145736 | tf_op jit(solution)/shard_map/gather_one/ppermute | solution.py:239
  95.1 2.3 collective-permute-done.1.other_ref
  97.3 0.0 copy-done.3
  97.3 0.0 copy-done.4
  97.3 3.8 %product_one.1 = bf16[16,288,128]{2,1,0:T(8,128)(2,1)S(1)} custom-call(s32[1]{0:T(128)} %bitcast.core_ref, s32[32]{0:T(128)S(1)} %copy-done.4, s32[32]{0:T(128)S(1)} %copy-done.3, s32[1]{0:T(128)S(6)} %copy.6.live_ref, bf16[32,256,256]{2,1,0:T(8,128)(2,1)} %tiles_ref.5, bf16[16,256,128]{2,1,0:T(8,128)(2,1)S(1)} %all_to_all.40.mine_ref, ...), custom_call_target="tpu_custom_call" | custom-call | tf_op jit(solution)/shard_map/product_one/pallas_call | solution.py:242
  101.1 27.0 %all_to_all.41.arrived_ref = bf16[16,288,128]{2,1,0:T(8,128)(2,1)S(1)} all-to-all(bf16[16,288,128]{2,1,0:T(8,128)(2,1)S(1)} %product_one.1), channel_id=1, replica_groups=mesh['z'=16,'core'=2,'x'=4,'y'=4] {'x','y'}, dimensions={0} | all-to-all | bytes 2359296 | tf_op jit(solution)/shard_map/reduce_one/all_to_all | solution.py:256
  128.2 0.5 middle.1
  128.7 61.6 %all_to_all.42.mine_ref = bf16[16,288,128]{2,1,0:T(8,128)(2,1)S(1)} all-to-all(bf16[16,288,128]{2,1,0:T(8,128)(2,1)S(1)} %get-tuple-element.14), channel_id=1, replica_groups=mesh['z'=16,'core'=2,'x'=4,'y'=4] {'z'}, dimensions={0} | all-to-all | bytes 2359296 | tf_op jit(solution)/shard_map/gather_two/all_to_all | solution.py:238
  190.2 5.9 %collective-permute-start.2 = (bf16[16,288,128]{2,1,0:T(8,128)(2,1)S(1)}, bf16[16,288,128]{2,1,0:T(8,128)(2,1)S(1)}, u32[]{:S(2)}, u32[]{:S(2)}) collective-permute-start(bf16[16,288,128]{2,1,0:T(8,128)(2,1)S(1)} %all_to_all.42.mine_ref), channel_id=1, source_target_pairs={{0,16},{16,0},{1,17},{17,1},{2,18},{18,2},{3,19},{19,3},{4,20},{20... | collective-permute-start | bytes 3538952 | tf_op jit(solution)/shard_map/gather_two/ppermute | solution.py:239
  196.1 2.5 collective-permute-done.2.other_ref
  198.6 3.6 %product_two.1 = bf16[16,288,128]{2,1,0:T(8,128)(2,1)S(1)} custom-call(s32[1]{0:T(128)} %bitcast.core_ref, s32[32]{0:T(128)S(1)} %copy-done.4, s32[32]{0:T(128)S(1)} %copy-done.3, s32[1]{0:T(128)S(6)} %copy.6.live_ref, bf16[32,256,256]{2,1,0:T(8,128)(2,1)} %tiles_ref.5, bf16[16,288,128]{2,1,0:T(8,128)(2,1)S(1)} %all_to_all.42.mine_ref, ...), custom_call_target="tpu_custom_call" | custom-call | tf_op jit(solution)/shard_map/product_two/pallas_call | solution.py:242
  202.2 23.1 %all_to_all.43.arrived_ref = bf16[16,288,128]{2,1,0:T(8,128)(2,1)S(1)} all-to-all(bf16[16,288,128]{2,1,0:T(8,128)(2,1)S(1)} %product_two.1), channel_id=1, replica_groups=mesh['z'=16,'core'=2,'x'=4,'y'=4] {'x','y'}, dimensions={0} | all-to-all | bytes 2359296 | tf_op jit(solution)/shard_map/reduce_two/all_to_all | solution.py:270
  225.2 0.5 last.1
  225.7 11.9 %all_to_all.44 = f32[32,4,128]{2,1,0:T(4,128)S(1)} all-to-all(f32[32,4,128]{2,1,0:T(4,128)S(1)} %bitcast.6), channel_id=1, replica_groups=mesh['z'=16,'core'=2,'x'=4,'y'=4] {'core','x','y'}, dimensions={0} | all-to-all | bytes 131072 | tf_op jit(solution)/shard_map/gram/all_to_all | solution.py:284
  237.7 16.1 %all_to_all.45 = f32[16,12,128]{2,1,0:T(8,128)S(1)} all-to-all(f32[16,12,128]{2,1,0:T(8,128)S(1)} %broadcast_in_dim.7), channel_id=1, replica_groups=mesh['z'=16,'core'=2,'x'=4,'y'=4] {'z'}, dimensions={0} | all-to-all | bytes 196608 | tf_op jit(solution)/shard_map/gram/all_to_all | solution.py:288
  253.8 0.6 broadcast_in_dim.8
  254.5 7.2 %all-to-all-start.7 = ((f32[32,4,128]{2,1,0:T(4,128)}), f32[32,4,128]{2,1,0:T(4,128)S(1)}, u32[]{:S(2)}, u32[]{:S(2)}) async-start(f32[32,4,128]{2,1,0:T(4,128)} %broadcast_in_dim.8), calls=%async_computation.7 | async-start | bytes 131072 | tf_op jit(solution)/shard_map/gram/all_to_all | solution.py:292
  261.7 7.1 %all-to-all-done.7 = f32[32,4,128]{2,1,0:T(4,128)S(1)} async-done(((f32[32,4,128]{2,1,0:T(4,128)}), f32[32,4,128]{2,1,0:T(4,128)S(1)}, u32[]{:S(2)}, u32[]{:S(2)}) %all-to-all-start.7) | async-done | bytes 65568 | tf_op jit(solution)/shard_map/gram/all_to_all | solution.py:292
  268.8 35.8 %finish.1 = f32[256,128]{1,0:T(8,128)} custom-call(f32[128,128]{1,0:T(8,128)S(1)} %slice_bitcast_fusion.first_gram_ref, f32[128,128]{1,0:T(8,128)S(1)} %bitcast.5, f32[256,128]{1,0:T(8,128)S(1)} %get-tuple-element.18.fresh_ref), custom_call_target="tpu_custom_call" | custom-call | tf_op jit(solution)/shard_map/finish/pallas_call | solution.py:294
  (9 shorter events, 0.1 us)
Async XLA Ops:
  0.7 2.2 copy-start
  2.8 0.7 copy-start.2
  3.5 34.3 %copy-start.1 = (bf16[256,128]{1,0:T(8,128)(2,1)S(1)}, bf16[256,128]{1,0:T(8,128)(2,1)}, u32[]{:S(2)}) copy-start(bf16[256,128]{1,0:T(8,128)(2,1)} %initial_ref.1) | copy-start | bytes 196612
  5.3 92.0 %copy-start.3 = (s32[32]{0:T(128)S(1)}, s32[32]{0:T(128)}, u32[]{:S(2)}) copy-start(s32[32]{0:T(128)} %cols_ref.5) | copy-start | bytes 388
  5.3 92.0 %copy-start.4 = (s32[32]{0:T(128)S(1)}, s32[32]{0:T(128)}, u32[]{:S(2)}) copy-start(s32[32]{0:T(128)} %rows_ref.3) | copy-start | bytes 388
  5.3 27.6 %all-to-all-start = ((f32[16,8,128]{2,1,0:T(8,128)}), f32[16,8,128]{2,1,0:T(8,128)S(1)}, u32[]{:S(2)}, u32[]{:S(2)}) async-start(f32[16,8,128]{2,1,0:T(8,128)} %col_degree.1), calls=%async_computation | async-start | bytes 131072 | tf_op jit(solution)/shard_map/col_degree/all_to_all | solution.py:225
  32.9 4.9 %collective-permute-start = (f32[2,128]{1,0:T(2,128)S(1)}, f32[2,128]{1,0:T(2,128)S(1)}, u32[]{:S(2)}, u32[]{:S(2)}) collective-permute-start(f32[2,128]{1,0:T(2,128)S(1)} %get-tuple-element.19), channel_id=1, source_target_pairs={{0,16},{16,0},{1,17},{17,1},{2,18},{18,2},{3,19},{19,3},{4,20},{20... | collective-permute-start | bytes 3080 | tf_op jit(solution)/shard_map/col_degree/ppermute | solution.py:227
  85.7 11.6 %collective-permute-start.1 = (bf16[16,256,128]{2,1,0:T(8,128)(2,1)S(1)}, bf16[16,256,128]{2,1,0:T(8,128)(2,1)S(1)}, u32[]{:S(2)}, u32[]{:S(2)}) collective-permute-start(bf16[16,256,128]{2,1,0:T(8,128)(2,1)S(1)} %all_to_all.40.mine_ref), channel_id=1, source_target_pairs={{0,16},{16,0},{1,17},{17,1},{2,18},{18,2},{3,19},{19,3},{4,20},{20... | collective-permute-start | bytes 3145736 | tf_op jit(solution)/shard_map/gather_one/ppermute | solution.py:239
  190.2 8.3 %collective-permute-start.2 = (bf16[16,288,128]{2,1,0:T(8,128)(2,1)S(1)}, bf16[16,288,128]{2,1,0:T(8,128)(2,1)S(1)}, u32[]{:S(2)}, u32[]{:S(2)}) collective-permute-start(bf16[16,288,128]{2,1,0:T(8,128)(2,1)S(1)} %all_to_all.42.mine_ref), channel_id=1, source_target_pairs={{0,16},{16,0},{1,17},{17,1},{2,18},{18,2},{3,19},{19,3},{4,20},{20... | collective-permute-start | bytes 3538952 | tf_op jit(solution)/shard_map/gather_two/ppermute | solution.py:239
  254.5 14.4 %all-to-all-start.7 = ((f32[32,4,128]{2,1,0:T(4,128)}), f32[32,4,128]{2,1,0:T(4,128)S(1)}, u32[]{:S(2)}, u32[]{:S(2)}) async-start(f32[32,4,128]{2,1,0:T(4,128)} %broadcast_in_dim.8), calls=%async_computation.7 | async-start | bytes 131072 | tf_op jit(solution)/shard_map/gram/all_to_all | solution.py:292

commit v2 on v1

v2 whole, which is shorter than its diff:
```python
import functools

import jax
import jax.numpy as jnp
import numpy as np
from jax import lax
from jax.experimental import pallas as pl
from jax.experimental.pallas import tpu as pltpu
from jax.sharding import Mesh, PartitionSpec as P

ZS = 16
PEERS = 16
SIDE = 256
WIDTH = 128
FIRST = 16
SLOTS = 32
GROUP = 16
EXTRA = 16
GRAM_ROWS = 4
VMEM_BYTES = 24 * 1024 * 1024
F32 = jnp.float32
BF16 = jnp.bfloat16
HIGHEST = lax.Precision.HIGHEST

params = pltpu.CompilerParams(vmem_limit_bytes=VMEM_BYTES)
smem = pl.BlockSpec(memory_space=pltpu.SMEM)
vmem = pl.BlockSpec(memory_space=pltpu.VMEM)


def eye_mask():
    return lax.broadcasted_iota(jnp.int32, (WIDTH, WIDTH), 0) == lax.broadcasted_iota(
        jnp.int32, (WIDTH, WIDTH), 1
    )


def to_column(lanes):
    spread = jnp.broadcast_to(lanes, (WIDTH, WIDTH))
    return jnp.sum(jnp.where(eye_mask(), spread, 0.0), axis=1, keepdims=True)


def split3(value):
    high = value.astype(BF16)
    rest = value - high.astype(F32)
    middle = rest.astype(BF16)
    low = (rest - middle.astype(F32)).astype(BF16)
    return high, middle, low


def degree_kernel(cols_ref, live_ref, tiles_ref, out_ref, acc_ref):
    acc_ref[...] = jnp.zeros_like(acc_ref)

    def one(slot, carry):
        tile = tiles_ref[slot].astype(F32).reshape(SIDE // 8, 8, SIDE)
        acc_ref[cols_ref[slot]] += jnp.sum(tile, axis=0)
        return carry

    lax.fori_loop(0, live_ref[0], one, 0)
    out_ref[...] = jnp.zeros_like(out_ref)
    for block in range(2 * ZS):
        total = jnp.sum(acc_ref[block], axis=0, keepdims=True)
        at = 2 * (block % 2)
        out_ref[block // 2, at : at + 1, :] = total[:, :WIDTH]
        out_ref[block // 2, at + 1 : at + 2, :] = total[:, WIDTH:]


def scale_kernel(mine_ref, other_ref, initial_ref, out_ref, scale_ref):
    degree = mine_ref[...] + other_ref[...]
    scale = lax.rsqrt(degree)
    scale_ref[...] = scale
    for half in range(2):
        rows = slice(half * WIDTH, (half + 1) * WIDTH)
        column = to_column(scale[half : half + 1])
        out_ref[rows] = (column * initial_ref[rows].astype(F32)).astype(BF16)


def product_kernel(with_rows, place_ref, rows_ref, cols_ref, live_ref, tiles_ref, *refs):
    *parts, out_ref, acc_ref = refs
    live = live_ref[0]

    def product(slot):
        col = cols_ref[slot]
        core, level = lax.rem(col, 2), lax.div(col, 2)
        odd, at = lax.rem(level, 2), lax.div(level, 2)
        same_core, same_odd = core == place_ref[0], odd == place_ref[1]
        near = jnp.where(same_odd, parts[0][at], parts[1][at])
        far = jnp.where(same_odd, parts[2][at], parts[3][at])
        block = jnp.where(same_core, near, far)
        if with_rows:
            block = jnp.concatenate([block, jnp.ones((SIDE, WIDTH), BF16)], axis=1)
        block = jnp.where(slot < live, block, jnp.zeros_like(block))
        return jnp.dot(tiles_ref[slot], block, preferred_element_type=F32)

    def first(turn, carry):
        slots = [turn * GROUP + at for at in range(GROUP)]
        for slot, value in zip(slots, [product(slot) for slot in slots]):
            acc_ref[rows_ref[slot]] = value
        return carry

    def later(turn, carry):
        slots = [turn * GROUP + at for at in range(GROUP)]
        for slot, value in zip(slots, [product(slot) for slot in slots]):
            acc_ref[rows_ref[slot]] += value
        return carry

    lax.fori_loop(0, FIRST // GROUP, first, 0)
    lax.fori_loop(FIRST // GROUP, SLOTS // GROUP, later, 0)
    if with_rows:
        eye = eye_mask()
        zero = jnp.zeros((EXTRA - 6, WIDTH), BF16)
        for block in range(PEERS):
            out_ref[block, :SIDE] = acc_ref[block, :, :WIDTH].astype(BF16)
            pieces = []
            for half in range(2):
                spread = acc_ref[block, half * WIDTH : (half + 1) * WIDTH, WIDTH:]
                pieces.append(jnp.sum(jnp.where(eye, spread, 0.0), axis=0, keepdims=True))
            three = split3(jnp.concatenate(pieces, axis=0))
            out_ref[block, SIDE:] = jnp.concatenate(list(three) + [zero], axis=0)
    else:
        for block in range(PEERS):
            out_ref[block] = acc_ref[block].astype(BF16)


def total_of(ref, rows):
    total = ref[0, rows].astype(F32)
    for peer in range(1, PEERS):
        total += ref[peer, rows].astype(F32)
    return total


def gram_of(fresh):
    return lax.dot_general(
        fresh, fresh, (((0,), (0,)), ((), ())), precision=HIGHEST, preferred_element_type=F32
    )


def middle_kernel(arrived_ref, col_scale_ref, out_ref, row_scale_ref, gram_ref):
    extra = total_of(arrived_ref, slice(SIDE, SIDE + EXTRA))
    degree = extra[0:2] + extra[2:4] + extra[4:6]
    row_scale = lax.rsqrt(degree)
    row_scale_ref[...] = row_scale
    halves = []
    for half in range(2):
        rows = slice(half * WIDTH, (half + 1) * WIDTH)
        fresh = to_column(row_scale[half : half + 1]) * total_of(arrived_ref, rows)
        halves.append(fresh)
        out_ref[rows] = (to_column(col_scale_ref[half : half + 1]) * fresh).astype(BF16)
    gram_ref[...] = gram_of(jnp.concatenate(halves, axis=0))


def last_kernel(arrived_ref, row_scale_ref, first_gram_ref, fresh_ref, out_ref):
    halves = []
    for half in range(2):
        rows = slice(half * WIDTH, (half + 1) * WIDTH)
        fresh = to_column(row_scale_ref[half : half + 1]) * total_of(arrived_ref, rows)
        fresh_ref[rows] = fresh
        halves.append(fresh)
    gram = gram_of(jnp.concatenate(halves, axis=0))
    for peer in range(2 * PEERS):
        rows = slice(GRAM_ROWS * peer, GRAM_ROWS * (peer + 1))
        out_ref[peer, :GRAM_ROWS] = first_gram_ref[rows]
        out_ref[peer, GRAM_ROWS:] = gram[rows]


def lower_inverse(matrix):
    groups = WIDTH // 8
    parts = [matrix[8 * g : 8 * g + 8] for g in range(groups)]
    lane = lax.broadcasted_iota(jnp.int32, (8, WIDTH), 1)
    row = lax.broadcasted_iota(jnp.int32, (8, WIDTH), 0)
    out = []
    for g in range(groups):
        at = 8 * g
        panel = parts[g]
        inside = (lane >= at) & (lane < at + 8)
        cols = [jnp.broadcast_to(panel[:, at + j : at + j + 1], (8, WIDTH)) for j in range(8)]
        left = {}
        rows = []
        for i in range(8):
            for j in range(i + 1):
                left[i, j] = jnp.broadcast_to(cols[j][i : i + 1], (8, WIDTH))
            unit = jnp.where(lane == at + i, 1.0, 0.0)
            rows.append(jnp.where(inside, unit, jnp.broadcast_to(panel[i : i + 1], (8, WIDTH))))
        inverse, lower = [], {}
        for p in range(8):
            inverse.append(1.0 / left[p, p])
            for i in range(p + 1, 8):
                lower[i, p] = left[i, p] * inverse[p]
            for i in range(p + 1, 8):
                for j in range(p + 1, i + 1):
                    left[i, j] = left[i, j] - lower[i, p] * left[j, p]
                rows[i] = rows[i] - lower[i, p] * rows[p]
        total = jnp.zeros((8, WIDTH), F32)
        for i in range(8):
            total = jnp.where(row == i, rows[i] * lax.rsqrt(left[i, i]), total)
        out.append(jnp.where(lane <= row + at, total, 0.0))
        solved = {}
        for i in reversed(range(8)):
            solved[i] = rows[i] * inverse[i]
            for j in range(7, i, -1):
                solved[i] = solved[i] - lower[j, i] * solved[j]
        for h in range(g + 1, groups):
            even, odd = jnp.where(inside, 0.0, parts[h]), jnp.zeros((8, WIDTH), F32)
            for j in range(8):
                term = jnp.broadcast_to(parts[h][:, at + j : at + j + 1], (8, WIDTH)) * solved[j]
                if j % 2 == 0:
                    even = even - term
                else:
                    odd = odd + term
            parts[h] = even - odd
    return jnp.concatenate(out, axis=0)


def dot(a, b, dims):
    return lax.dot_general(a, b, (dims, ((), ())), precision=HIGHEST, preferred_element_type=F32)


def finish_kernel(grams_ref, fresh_ref, out_ref):
    first_gram = grams_ref[:, :GRAM_ROWS].reshape(WIDTH, WIDTH)
    gram = grams_ref[:, GRAM_ROWS:].reshape(WIDTH, WIDTH)
    first = lower_inverse(first_gram)
    gram = dot(dot(first, gram, ((1,), (0,))), first, ((1,), (1,)))
    second = lower_inverse(gram)
    fresh = dot(fresh_ref[...], first, ((1,), (1,)))
    out_ref[...] = dot(fresh, second, ((1,), (1,)))


def shape(dims, dtype):
    return jax.ShapeDtypeStruct(dims, dtype)


def shards(tile_values, tile_rows, tile_cols, live_count, initial):
    core = lax.axis_index("core")
    odd = lax.axis_index("odd")
    place = jnp.stack([core, odd]).astype(jnp.int32)
    levels = ("level", "odd")
    plane = ("core", "x", "y")
    swap = [(0, 1), (1, 0)]

    with jax.named_scope("col_degree"):
        part = pl.pallas_call(
            degree_kernel,
            out_shape=shape((ZS, 8, WIDTH), F32),
            in_specs=[smem, smem, vmem],
            out_specs=vmem,
            scratch_shapes=[pltpu.VMEM((2 * ZS, 8, SIDE), F32)],
            compiler_params=params,
        )(tile_cols, live_count, tile_values)
        pieces = jnp.sum(lax.all_to_all(part, levels, 0, 0, tiled=True), axis=0)
        mine = lax.dynamic_slice_in_dim(pieces, 2 * core, 2, 0)
        other = lax.ppermute(lax.dynamic_slice_in_dim(pieces, 2 - 2 * core, 2, 0), "core", swap)
    with jax.named_scope("scale"):
        sent, col_scale = pl.pallas_call(
            scale_kernel,
            out_shape=(shape((SIDE, WIDTH), BF16), shape((2, WIDTH), F32)),
            in_specs=[vmem] * 3,
            out_specs=(vmem, vmem),
            compiler_params=params,
        )(mine, other, initial)

    def gather(sent):
        mine = lax.all_gather(sent, "level", axis=0)
        beside = lax.ppermute(mine, "odd", swap)
        return mine, beside, lax.ppermute(mine, "core", swap), lax.ppermute(beside, "core", swap)

    def product(with_rows, parts):
        extra, width = (EXTRA, 2 * WIDTH) if with_rows else (0, WIDTH)
        return pl.pallas_call(
            functools.partial(product_kernel, with_rows),
            out_shape=shape((PEERS, SIDE + extra, WIDTH), BF16),
            in_specs=[smem] * 4 + [vmem] * 5,
            out_specs=vmem,
            scratch_shapes=[pltpu.VMEM((PEERS, SIDE, width), F32)],
            compiler_params=params,
        )(place, tile_rows, tile_cols, live_count, tile_values, *parts)

    with jax.named_scope("gather_one"):
        parts = gather(sent)
    with jax.named_scope("product_one"):
        partial_value = product(True, parts)
    with jax.named_scope("reduce_one"):
        arrived = lax.all_to_all(partial_value, ("x", "y"), 0, 0, tiled=True)
    with jax.named_scope("middle"):
        sent, row_scale, first_gram = pl.pallas_call(
            middle_kernel,
            out_shape=(shape((SIDE, WIDTH), BF16), shape((2, WIDTH), F32), shape((WIDTH, WIDTH), F32)),
            in_specs=[vmem] * 2,
            out_specs=(vmem,) * 3,
            compiler_params=params,
        )(arrived, col_scale)
    with jax.named_scope("gather_two"):
        parts = gather(sent)
    with jax.named_scope("product_two"):
        partial_value = product(False, parts)
    with jax.named_scope("reduce_two"):
        arrived = lax.all_to_all(partial_value, ("x", "y"), 0, 0, tiled=True)
    with jax.named_scope("last"):
        count, deep = 2 * PEERS, 2 * GRAM_ROWS
        fresh, grams = pl.pallas_call(
            last_kernel,
            out_shape=(shape((SIDE, WIDTH), F32), shape((count, deep, WIDTH), F32)),
            in_specs=[vmem] * 3,
            out_specs=(vmem,) * 2,
            compiler_params=params,
        )(arrived, row_scale, first_gram)
    with jax.named_scope("gram"):
        piece = jnp.sum(lax.all_to_all(grams, plane, 0, 0, tiled=True), axis=0)
        spread = jnp.broadcast_to(piece[None], (ZS, deep, WIDTH))
        piece = jnp.sum(lax.all_to_all(spread, levels, 0, 0, tiled=True), axis=0)
        spread = jnp.broadcast_to(piece[None], (count, deep, WIDTH))
        grams = lax.all_to_all(spread, plane, 0, 0, tiled=True)
    with jax.named_scope("finish"):
        return pl.pallas_call(
            finish_kernel,
            out_shape=shape((SIDE, WIDTH), F32),
            in_specs=[vmem] * 2,
            out_specs=vmem,
            compiler_params=params,
        )(grams, fresh)


def solution(mesh):
    devices = np.asarray(mesh.devices).reshape(ZS // 2, 2, 2, 4, 4)
    whole = ("level", "odd", "core", "x", "y")
    fine = Mesh(devices, whole)
    in_specs = (P(whole, None, None), P(whole), P(whole), P(whole), P(whole, None))
    return jax.shard_map(
        shards, mesh=fine, in_specs=in_specs, out_specs=P(whole, None), check_vma=False
    )
```

time: 305 us -> 235 us (0.77)
  blocking collectives: 187 us -> 134 us
  Pallas kernels: 46.1 us -> 19.6 us
  starting transfers between devices: 42.5 us -> 59.8 us
  waiting for transfers between devices: 24.2 us -> 15.3 us
    all_to_all x4 -> x3, blocking collectives: 137 us -> 42.6 us  [the longest x1 16.8 us: shards(): piece = jnp.sum(lax.all_to_all(spread, levels, 0, 0, tiled=True), axis=0)]
    all_gather x0 -> x2, blocking collectives: none -> 48.9 us  [gather(): mine = lax.all_gather(sent, 'level', axis=0)]
    ppermute x2 -> x6, starting transfers between devices: 15.2 us -> 39.9 us  [the longest x2 18.1 us: gather(): lax.ppermute(mine, 'core', swap)]
    pallas_call x1, Pallas kernels: 35.8 us -> 11.3 us  [shards(): pl.pallas_call(finish_kernel, out_shape=shape((SIDE, WIDTH), F32), in_spe...]
    all_to_all x2 -> x1, starting transfers between devices: 23.2 us -> 15.5 us  [shards(): pieces = jnp.sum(lax.all_to_all(part, levels, 0, 0, tiled=True), axis=0)]
    all_to_all x2, blocking collectives: 50.1 us -> 42.5 us  [shards(): arrived = lax.all_to_all(partial_value, ('x', 'y'), 0, 0, tiled=True)]
    all_to_all x2 -> x1, waiting for transfers between devices: 18.6 us -> 11.6 us  [shards(): pieces = jnp.sum(lax.all_to_all(part, levels, 0, 0, tiled=True), axis=0)]
  transfers between devices with their start and end apart: 5 -> 8, of which waited for: 5 -> 4; matrix products, arithmetic and copies ran while one was open for 0% -> 0% of each run, Pallas kernels for 0% -> 0%
where the time goes in v2:
time: 235 us
  blocking collectives  134 us (57%)
  starting transfers between devices  59.8 us (25%)
  Pallas kernels  19.6 us (8%)
  waiting for transfers between devices  15.3 us (7%)
  local copies, waits for them, and re-layouts  5.07 us (2%)
    all_gather x2, blocking collectives, gather(): mine = lax.all_gather(sent, 'level', axis=0)  48.9 us
    all_to_all x2, blocking collectives, shards(): arrived = lax.all_to_all(partial_value, ('x', 'y'), 0, 0, tiled=True)  42.5 us
    ppermute x2, starting transfers between devices, gather(): lax.ppermute(mine, 'core', swap)  18.1 us
    ppermute x2, starting transfers between devices, gather(): lax.ppermute(beside, 'core', swap)  17.8 us
    all_to_all x1, blocking collectives, shards(): piece = jnp.sum(lax.all_to_all(spread, levels, 0, 0, tiled=True), axis=0)  16.8 us
    all_to_all x1, starting transfers between devices, shards(): pieces = jnp.sum(lax.all_to_all(part, levels, 0, 0, tiled=True), axis=0)  15.5 us
    all_to_all x1, blocking collectives, shards(): grams = lax.all_to_all(spread, plane, 0, 0, tiled=True)  13 us
    all_to_all x1, blocking collectives, shards(): piece = jnp.sum(lax.all_to_all(grams, plane, 0, 0, tiled=True), axis=0)  12.8 us
  transfers between devices with their start and end apart: 8, of which 4 were waited for; matrix products, arithmetic and copies ran while one was open for 0% of the time, Pallas kernels for 0%

profile of v2, /device:TPU:1, one launch (start us, length us, event | category | flops | bytes accessed | tf_op | source)
XLA Modules:
  0.0 234.8 jit_solution(3834388571784026593)
XLA Ops:
  0.7 0.0 copy-start
  0.7 2.2 copy-done
  2.8 0.7 copy-done.4
  3.5 2.3 col_degree.1
  5.8 15.5 %all-to-all-start = ((f32[16,8,128]{2,1,0:T(8,128)}), f32[16,8,128]{2,1,0:T(8,128)S(1)}, u32[]{:S(2)}, u32[]{:S(2)}) async-start(f32[16,8,128]{2,1,0:T(8,128)} %col_degree.1), calls=%async_computation | async-start | bytes 131072 | tf_op jit(solution)/shard_map/col_degree/all_to_all | solution.py:247
  21.3 11.6 %all-to-all-done = f32[16,8,128]{2,1,0:T(8,128)S(1)} async-done(((f32[16,8,128]{2,1,0:T(8,128)}), f32[16,8,128]{2,1,0:T(8,128)S(1)}, u32[]{:S(2)}, u32[]{:S(2)}) %all-to-all-start) | async-done | bytes 65568 | tf_op jit(solution)/shard_map/col_degree/all_to_all | solution.py:247
  32.9 4.5 %collective-permute-start = (f32[2,128]{1,0:T(2,128)S(1)}, f32[2,128]{1,0:T(2,128)S(1)}, u32[]{:S(2)}, u32[]{:S(2)}) collective-permute-start(f32[2,128]{1,0:T(2,128)S(1)} %get-tuple-element.19), channel_id=1, source_target_pairs={{0,16},{16,0},{1,17},{17,1},{2,18},{18,2},{3,19},{19,3},{4,20},{20... | collective-permute-start | bytes 3080 | tf_op jit(solution)/shard_map/col_degree/ppermute | solution.py:249
  37.4 0.8 collective-permute-done.other_ref
  38.2 0.1 scale.1
  38.3 24.8 %all-gather = bf16[2048,128]{1,0:T(8,128)(2,1)S(1)} all-gather(bf16[256,128]{1,0:T(8,128)(2,1)S(1)} %get-tuple-element.12), channel_id=2, replica_groups=mesh['level'=8,'odd'=2,'core'=2,'x'=4,'y'=4] {'level'}, dimensions={0}, use_global_device_ids=true | all-gather | bytes 589824 | tf_op jit(solution)/shard_map/gather_one/all_gather | solution.py:260
  63.2 2.0 collective-permute-start.1
  65.2 7.9 %collective-permute-start.2 = (bf16[8,256,128]{2,1,0:T(8,128)(2,1)S(1)}, bf16[8,256,128]{2,1,0:T(8,128)(2,1)S(1)}, u32[]{:S(2)}, u32[]{:S(2)}) collective-permute-start(bf16[8,256,128]{2,1,0:T(8,128)(2,1)S(1)} %bitcast.5), channel_id=1, source_target_pairs={{0,16},{16,0},{1,17},{17,1},{2,18},{18,2},{3,19},{19,3},{4,20},{20... | collective-permute-start | bytes 1572872 | tf_op jit(solution)/shard_map/gather_one/ppermute | solution.py:262
  73.2 8.7 %collective-permute-start.3 = (bf16[8,256,128]{2,1,0:T(8,128)(2,1)S(1)}, bf16[8,256,128]{2,1,0:T(8,128)(2,1)S(1)}, u32[]{:S(2)}, u32[]{:S(2)}) collective-permute-start(bf16[8,256,128]{2,1,0:T(8,128)(2,1)S(1)} %collective-permute-done.1.refs_1_), channel_id=1, source_target_pairs={{0,16},{16,0},{1,17},{17,1},{2,18},{18,2},{3,19},{19,3},{4,20},{20... | collective-permute-start | bytes 1572872 | tf_op jit(solution)/shard_map/gather_one/ppermute | solution.py:262
  81.9 0.1 pad_add_fusion.place_ref
  82.0 1.4 collective-permute-done.3.refs_3_
  83.4 2.2 copy-done.1
  85.6 2.7 %product_one.1 = bf16[16,272,128]{2,1,0:T(8,128)(2,1)S(1)} custom-call(s32[2]{0:T(128)S(1)} %pad_add_fusion.place_ref, s32[32]{0:T(128)S(1)} %copy-done.6, s32[32]{0:T(128)S(1)} %copy-done.5, s32[1]{0:T(128)S(6)} %copy.6.live_ref, bf16[32,256,256]{2,1,0:T(8,128)(2,1)S(1)} %copy-done.1, bf16[8,256,128]{2,1,0:T(8,128)(2,1)S(1)} %bitcast.6, ...), custom_call_target="tpu_custom_call" | custom-call | tf_op jit(solution)/shard_map/product_one/pallas_call | solution.py:266
  88.3 23.7 %all_to_all.30.arrived_ref = bf16[16,272,128]{2,1,0:T(8,128)(2,1)S(1)} all-to-all(bf16[16,272,128]{2,1,0:T(8,128)(2,1)S(1)} %product_one.1), channel_id=1, replica_groups=mesh['level'=8,'odd'=2,'core'=2,'x'=4,'y'=4] {'x','y'}, dimensions={0} | all-to-all | bytes 2228224 | tf_op jit(solution)/shard_map/reduce_one/all_to_all | solution.py:280
  112.0 0.5 middle.1
  112.5 24.1 %all-gather.1 = bf16[2048,128]{1,0:T(8,128)(2,1)S(1)} all-gather(bf16[256,128]{1,0:T(8,128)(2,1)S(1)} %get-tuple-element.14), channel_id=3, replica_groups=mesh['level'=8,'odd'=2,'core'=2,'x'=4,'y'=4] {'level'}, dimensions={0}, use_global_device_ids=true | all-gather | bytes 589824 | tf_op jit(solution)/shard_map/gather_two/all_gather | solution.py:260
  136.6 1.9 collective-permute-start.4
  138.5 10.2 %collective-permute-start.5 = (bf16[8,256,128]{2,1,0:T(8,128)(2,1)S(1)}, bf16[8,256,128]{2,1,0:T(8,128)(2,1)S(1)}, u32[]{:S(2)}, u32[]{:S(2)}) collective-permute-start(bf16[8,256,128]{2,1,0:T(8,128)(2,1)S(1)} %bitcast.8), channel_id=1, source_target_pairs={{0,16},{16,0},{1,17},{17,1},{2,18},{18,2},{3,19},{19,3},{4,20},{20... | collective-permute-start | bytes 1572872 | tf_op jit(solution)/shard_map/gather_two/ppermute | solution.py:262
  148.7 9.1 %collective-permute-start.6 = (bf16[8,256,128]{2,1,0:T(8,128)(2,1)S(1)}, bf16[8,256,128]{2,1,0:T(8,128)(2,1)S(1)}, u32[]{:S(2)}, u32[]{:S(2)}) collective-permute-start(bf16[8,256,128]{2,1,0:T(8,128)(2,1)S(1)} %collective-permute-done.4.refs_1_), channel_id=1, source_target_pairs={{0,16},{16,0},{1,17},{17,1},{2,18},{18,2},{3,19},{19,3},{4,20},{20... | collective-permute-start | bytes 1572872 | tf_op jit(solution)/shard_map/gather_two/ppermute | solution.py:262
  157.8 0.0 collective-permute-done.5.refs_2_
  157.8 1.5 collective-permute-done.6.refs_3_
  159.3 2.3 product_two.1
  161.6 18.7 %all_to_all.31.arrived_ref = bf16[16,256,128]{2,1,0:T(8,128)(2,1)S(1)} all-to-all(bf16[16,256,128]{2,1,0:T(8,128)(2,1)S(1)} %product_two.1), channel_id=1, replica_groups=mesh['level'=8,'odd'=2,'core'=2,'x'=4,'y'=4] {'x','y'}, dimensions={0} | all-to-all | bytes 2097152 | tf_op jit(solution)/shard_map/reduce_two/all_to_all | solution.py:294
  180.3 0.5 last.1
  180.8 12.8 %all_to_all.32 = f32[32,8,128]{2,1,0:T(8,128)S(1)} all-to-all(f32[32,8,128]{2,1,0:T(8,128)S(1)} %get-tuple-element.17), channel_id=1, replica_groups=mesh['level'=8,'odd'=2,'core'=2,'x'=4,'y'=4] {'core','x','y'}, dimensions={0} | all-to-all | bytes 262144 | tf_op jit(solution)/shard_map/gram/all_to_all | solution.py:305
  193.7 16.8 %all_to_all.33 = f32[16,8,128]{2,1,0:T(8,128)S(1)} all-to-all(f32[16,8,128]{2,1,0:T(8,128)S(1)} %broadcast_in_dim.4), channel_id=1, replica_groups=mesh['level'=8,'odd'=2,'core'=2,'x'=4,'y'=4] {'level','odd'}, dimensions={0} | all-to-all | bytes 131072 | tf_op jit(solution)/shard_map/gram/all_to_all | solution.py:307
  210.5 13.0 %all_to_all.34.grams_ref = f32[32,8,128]{2,1,0:T(8,128)S(1)} all-to-all(f32[32,8,128]{2,1,0:T(8,128)S(1)} %broadcast_in_dim.5), channel_id=1, replica_groups=mesh['level'=8,'odd'=2,'core'=2,'x'=4,'y'=4] {'core','x','y'}, dimensions={0} | all-to-all | bytes 262144 | tf_op jit(solution)/shard_map/gram/all_to_all | solution.py:309
  223.5 11.3 %finish.1 = f32[256,128]{1,0:T(8,128)} custom-call(f32[32,8,128]{2,1,0:T(8,128)S(1)} %all_to_all.34.grams_ref, f32[256,128]{1,0:T(8,128)S(1)} %get-tuple-element.18.fresh_ref), custom_call_target="tpu_custom_call" | custom-call | tf_op jit(solution)/shard_map/finish/pallas_call | solution.py:311
  (19 shorter events, 0.1 us)
Async XLA Ops:
  0.7 2.2 copy-start
  2.8 0.7 copy-start.4
  3.5 34.7 %copy-start.3 = (bf16[256,128]{1,0:T(8,128)(2,1)S(1)}, bf16[256,128]{1,0:T(8,128)(2,1)}, u32[]{:S(2)}) copy-start(bf16[256,128]{1,0:T(8,128)(2,1)} %initial_ref.1) | copy-start | bytes 196612
  3.5 79.9 %copy-start.5 = (s32[32]{0:T(128)S(1)}, s32[32]{0:T(128)}, u32[]{:S(2)}) copy-start(s32[32]{0:T(128)} %cols_ref.5) | copy-start | bytes 388
  3.5 79.9 %copy-start.6 = (s32[32]{0:T(128)S(1)}, s32[32]{0:T(128)}, u32[]{:S(2)}) copy-start(s32[32]{0:T(128)} %rows_ref.3) | copy-start | bytes 388
  5.8 27.1 %all-to-all-start = ((f32[16,8,128]{2,1,0:T(8,128)}), f32[16,8,128]{2,1,0:T(8,128)S(1)}, u32[]{:S(2)}, u32[]{:S(2)}) async-start(f32[16,8,128]{2,1,0:T(8,128)} %col_degree.1), calls=%async_computation | async-start | bytes 131072 | tf_op jit(solution)/shard_map/col_degree/all_to_all | solution.py:247
  32.9 5.3 %collective-permute-start = (f32[2,128]{1,0:T(2,128)S(1)}, f32[2,128]{1,0:T(2,128)S(1)}, u32[]{:S(2)}, u32[]{:S(2)}) collective-permute-start(f32[2,128]{1,0:T(2,128)S(1)} %get-tuple-element.19), channel_id=1, source_target_pairs={{0,16},{16,0},{1,17},{17,1},{2,18},{18,2},{3,19},{19,3},{4,20},{20... | collective-permute-start | bytes 3080 | tf_op jit(solution)/shard_map/col_degree/ppermute | solution.py:249
  63.2 10.0 %collective-permute-start.1 = (bf16[8,256,128]{2,1,0:T(8,128)(2,1)S(1)}, bf16[8,256,128]{2,1,0:T(8,128)(2,1)S(1)}, u32[]{:S(2)}, u32[]{:S(2)}) collective-permute-start(bf16[8,256,128]{2,1,0:T(8,128)(2,1)S(1)} %bitcast.4), channel_id=1, source_target_pairs={{0,32},{32,0},{1,33},{33,1},{2,34},{34,2},{3,35},{35,3},{4,36},{36... | collective-permute-start | bytes 1572872 | tf_op jit(solution)/shard_map/gather_one/ppermute | solution.py:261
  65.2 16.7 %collective-permute-start.2 = (bf16[8,256,128]{2,1,0:T(8,128)(2,1)S(1)}, bf16[8,256,128]{2,1,0:T(8,128)(2,1)S(1)}, u32[]{:S(2)}, u32[]{:S(2)}) collective-permute-start(bf16[8,256,128]{2,1,0:T(8,128)(2,1)S(1)} %bitcast.5), channel_id=1, source_target_pairs={{0,16},{16,0},{1,17},{17,1},{2,18},{18,2},{3,19},{19,3},{4,20},{20... | collective-permute-start | bytes 1572872 | tf_op jit(solution)/shard_map/gather_one/ppermute | solution.py:262
  73.2 10.2 %collective-permute-start.3 = (bf16[8,256,128]{2,1,0:T(8,128)(2,1)S(1)}, bf16[8,256,128]{2,1,0:T(8,128)(2,1)S(1)}, u32[]{:S(2)}, u32[]{:S(2)}) collective-permute-start(bf16[8,256,128]{2,1,0:T(8,128)(2,1)S(1)} %collective-permute-done.1.refs_1_), channel_id=1, source_target_pairs={{0,16},{16,0},{1,17},{17,1},{2,18},{18,2},{3,19},{19,3},{4,20},{20... | collective-permute-start | bytes 1572872 | tf_op jit(solution)/shard_map/gather_one/ppermute | solution.py:262
  83.4 2.2 copy-start.1
  85.6 73.8 %copy-start.2 = (bf16[32,256,256]{2,1,0:T(8,128)(2,1)S(1)}, bf16[32,256,256]{2,1,0:T(8,128)(2,1)}, u32[]{:S(2)}) copy-start(bf16[32,256,256]{2,1,0:T(8,128)(2,1)} %tiles_ref.5) | copy-start | bytes 12582916
  136.6 12.1 %collective-permute-start.4 = (bf16[8,256,128]{2,1,0:T(8,128)(2,1)S(1)}, bf16[8,256,128]{2,1,0:T(8,128)(2,1)S(1)}, u32[]{:S(2)}, u32[]{:S(2)}) collective-permute-start(bf16[8,256,128]{2,1,0:T(8,128)(2,1)S(1)} %bitcast.7), channel_id=1, source_target_pairs={{0,32},{32,0},{1,33},{33,1},{2,34},{34,2},{3,35},{35,3},{4,36},{36... | collective-permute-start | bytes 1572872 | tf_op jit(solution)/shard_map/gather_two/ppermute | solution.py:261
  138.5 19.3 %collective-permute-start.5 = (bf16[8,256,128]{2,1,0:T(8,128)(2,1)S(1)}, bf16[8,256,128]{2,1,0:T(8,128)(2,1)S(1)}, u32[]{:S(2)}, u32[]{:S(2)}) collective-permute-start(bf16[8,256,128]{2,1,0:T(8,128)(2,1)S(1)} %bitcast.8), channel_id=1, source_target_pairs={{0,16},{16,0},{1,17},{17,1},{2,18},{18,2},{3,19},{19,3},{4,20},{20... | collective-permute-start | bytes 1572872 | tf_op jit(solution)/shard_map/gather_two/ppermute | solution.py:262
  148.7 10.6 %collective-permute-start.6 = (bf16[8,256,128]{2,1,0:T(8,128)(2,1)S(1)}, bf16[8,256,128]{2,1,0:T(8,128)(2,1)S(1)}, u32[]{:S(2)}, u32[]{:S(2)}) collective-permute-start(bf16[8,256,128]{2,1,0:T(8,128)(2,1)S(1)} %collective-permute-done.4.refs_1_), channel_id=1, source_target_pairs={{0,16},{16,0},{1,17},{17,1},{2,18},{18,2},{3,19},{19,3},{4,20},{20... | collective-permute-start | bytes 1572872 | tf_op jit(solution)/shard_map/gather_two/ppermute | solution.py:262

commit v3 on v2

--- a/solution.py
+++ b/solution.py
@@ -9,12 +9,13 @@
 from jax.sharding import Mesh, PartitionSpec as P
 
 ZS = 16
+QUADS = 4
 PEERS = 16
 SIDE = 256
 WIDTH = 128
-FIRST = 16
 SLOTS = 32
 GROUP = 16
+DEGREE_PARTS = 4
 EXTRA = 16
 GRAM_ROWS = 4
 VMEM_BYTES = 24 * 1024 * 1024
@@ -23,8 +24,11 @@
 HIGHEST = lax.Precision.HIGHEST
 
 params = pltpu.CompilerParams(vmem_limit_bytes=VMEM_BYTES)
+degree_params = pltpu.CompilerParams(vmem_limit_bytes=61 * 1024 * 1024)
+product_params = pltpu.CompilerParams(vmem_limit_bytes=48 * 1024 * 1024)
 smem = pl.BlockSpec(memory_space=pltpu.SMEM)
 vmem = pl.BlockSpec(memory_space=pltpu.VMEM)
+hbm = pl.BlockSpec(memory_space=pl.ANY)
 
 
 def eye_mask():
@@ -46,15 +50,33 @@
     return high, middle, low
 
 
-def degree_kernel(cols_ref, live_ref, tiles_ref, out_ref, acc_ref):
+def tile_copies(parts, tiles_ref, held_ref, sems):
+    size = SLOTS // parts
+    copies = []
+    for part in range(parts):
+        rows = pl.ds(part * size, size)
+        copies.append(pltpu.make_async_copy(tiles_ref.at[rows], held_ref.at[rows], sems.at[part]))
+    return copies
+
+
+def degree_kernel(cols_ref, live_ref, tiles_ref, out_ref, held_ref, acc_ref, sems):
+    copies = tile_copies(DEGREE_PARTS, tiles_ref, held_ref, sems)
+    for copy in copies:
+        copy.start()
     acc_ref[...] = jnp.zeros_like(acc_ref)
+    size = SLOTS // DEGREE_PARTS
 
     def one(slot, carry):
-        tile = tiles_ref[slot].astype(F32).reshape(SIDE // 8, 8, SIDE)
-        acc_ref[cols_ref[slot]] += jnp.sum(tile, axis=0)
+        @pl.when(slot < live_ref[0])
+        def _():
+            tile = held_ref[slot].astype(F32).reshape(SIDE // 8, 8, SIDE)
+            acc_ref[cols_ref[slot]] += jnp.sum(tile, axis=0)
+
         return carry
 
-    lax.fori_loop(0, live_ref[0], one, 0)
+    for part, copy in enumerate(copies):
+        copy.wait()
+        lax.fori_loop(part * size, part * size + size, one, 0)
     out_ref[...] = jnp.zeros_like(out_ref)
     for block in range(2 * ZS):
         total = jnp.sum(acc_ref[block], axis=0, keepdims=True)
@@ -63,9 +85,9 @@
         out_ref[block // 2, at + 1 : at + 2, :] = total[:, WIDTH:]
 
 
-def scale_kernel(mine_ref, other_ref, initial_ref, out_ref, scale_ref):
-    degree = mine_ref[...] + other_ref[...]
-    scale = lax.rsqrt(degree)
+def scale_kernel(place_ref, pieces_ref, initial_ref, out_ref, scale_ref):
+    both = pieces_ref[0] + pieces_ref[1]
+    scale = lax.rsqrt(jnp.where(place_ref[0] == 0, both[0:2], both[2:4]))
     scale_ref[...] = scale
     for half in range(2):
         rows = slice(half * WIDTH, (half + 1) * WIDTH)
@@ -73,37 +95,35 @@
         out_ref[rows] = (column * initial_ref[rows].astype(F32)).astype(BF16)
 
 
-def product_kernel(with_rows, place_ref, rows_ref, cols_ref, live_ref, tiles_ref, *refs):
-    *parts, out_ref, acc_ref = refs
+def product_kernel(with_rows, place_ref, rows_ref, cols_ref, live_ref, tiles_ref, near_ref, far_ref, out_ref, acc_ref, *held):
     live = live_ref[0]
+    if with_rows:
+        held_ref, sems = held
+        copies = tile_copies(SLOTS // GROUP, tiles_ref, held_ref, sems)
+        for copy in copies:
+            copy.start()
+    else:
+        held_ref, copies = tiles_ref, []
 
     def product(slot):
         col = cols_ref[slot]
         core, level = lax.rem(col, 2), lax.div(col, 2)
-        odd, at = lax.rem(level, 2), lax.div(level, 2)
-        same_core, same_odd = core == place_ref[0], odd == place_ref[1]
-        near = jnp.where(same_odd, parts[0][at], parts[1][at])
-        far = jnp.where(same_odd, parts[2][at], parts[3][at])
-        block = jnp.where(same_core, near, far)
+        at = QUADS * lax.rem(level + QUADS - place_ref[1], QUADS) + lax.div(level, QUADS)
+        block = jnp.where(core == place_ref[0], near_ref[at], far_ref[at])
         if with_rows:
             block = jnp.concatenate([block, jnp.ones((SIDE, WIDTH), BF16)], axis=1)
         block = jnp.where(slot < live, block, jnp.zeros_like(block))
-        return jnp.dot(tiles_ref[slot], block, preferred_element_type=F32)
-
-    def first(turn, carry):
-        slots = [turn * GROUP + at for at in range(GROUP)]
+        return jnp.dot(held_ref[slot], block, preferred_element_type=F32)
+
+    for turn in range(SLOTS // GROUP):
+        if copies:
+            copies[turn].wait()
+        slots = range(turn * GROUP, (turn + 1) * GROUP)
         for slot, value in zip(slots, [product(slot) for slot in slots]):
-            acc_ref[rows_ref[slot]] = value
-        return carry
-
-    def later(turn, carry):
-        slots = [turn * GROUP + at for at in range(GROUP)]
-        for slot, value in zip(slots, [product(slot) for slot in slots]):
-            acc_ref[rows_ref[slot]] += value
-        return carry
-
-    lax.fori_loop(0, FIRST // GROUP, first, 0)
-    lax.fori_loop(FIRST // GROUP, SLOTS // GROUP, later, 0)
+            if turn == 0:
+                acc_ref[rows_ref[slot]] = value
+            else:
+                acc_ref[rows_ref[slot]] += value
     if with_rows:
         eye = eye_mask()
         zero = jnp.zeros((EXTRA - 6, WIDTH), BF16)
@@ -229,47 +249,61 @@
 
 def shards(tile_values, tile_rows, tile_cols, live_count, initial):
     core = lax.axis_index("core")
-    odd = lax.axis_index("odd")
-    place = jnp.stack([core, odd]).astype(jnp.int32)
-    levels = ("level", "odd")
+    place = jnp.stack([core, lax.axis_index("spot")]).astype(jnp.int32)
+    levels = ("quad", "spot")
     plane = ("core", "x", "y")
-    swap = [(0, 1), (1, 0)]
 
     with jax.named_scope("col_degree"):
         part = pl.pallas_call(
             degree_kernel,
             out_shape=shape((ZS, 8, WIDTH), F32),
-            in_specs=[smem, smem, vmem],
+            in_specs=[smem, smem, hbm],
             out_specs=vmem,
-            scratch_shapes=[pltpu.VMEM((2 * ZS, 8, SIDE), F32)],
-            compiler_params=params,
+            scratch_shapes=[
+                pltpu.VMEM(tile_values.shape, BF16),
+                pltpu.VMEM((2 * ZS, 8, SIDE), F32),
+                pltpu.SemaphoreType.DMA((DEGREE_PARTS,)),
+            ],
+            compiler_params=degree_params,
         )(tile_cols, live_count, tile_values)
         pieces = jnp.sum(lax.all_to_all(part, levels, 0, 0, tiled=True), axis=0)
-        mine = lax.dynamic_slice_in_dim(pieces, 2 * core, 2, 0)
-        other = lax.ppermute(lax.dynamic_slice_in_dim(pieces, 2 - 2 * core, 2, 0), "core", swap)
+        pieces = lax.all_gather(pieces, "core", axis=0)
     with jax.named_scope("scale"):
         sent, col_scale = pl.pallas_call(
             scale_kernel,
             out_shape=(shape((SIDE, WIDTH), BF16), shape((2, WIDTH), F32)),
-            in_specs=[vmem] * 3,
+            in_specs=[smem, vmem, vmem],
             out_specs=(vmem, vmem),
             compiler_params=params,
-        )(mine, other, initial)
+        )(place, pieces, initial)
+
+    def from_level(first, second):
+        steps = (first, second)
+        return [
+            (((z + steps[core]) % ZS) * 2 + core, z * 2 + core) for z in range(ZS) for core in range(2)
+        ]
 
     def gather(sent):
-        mine = lax.all_gather(sent, "level", axis=0)
-        beside = lax.ppermute(mine, "odd", swap)
-        return mine, beside, lax.ppermute(mine, "core", swap), lax.ppermute(beside, "core", swap)
+        chips = levels + ("core",)
+        mine = lax.all_gather(sent, "quad", axis=0)
+        two = lax.ppermute(mine, chips, from_level(2, -2))
+        one = lax.ppermute(mine, chips, from_level(1, 1))
+        three = lax.ppermute(mine, chips, from_level(-1, -1))
+        near = jnp.concatenate([mine, one, two, three], axis=0)
+        return near, lax.ppermute(near, "core", [(0, 1), (1, 0)])
 
     def product(with_rows, parts):
         extra, width = (EXTRA, 2 * WIDTH) if with_rows else (0, WIDTH)
+        scratch = [pltpu.VMEM((PEERS, SIDE, width), F32)]
+        if with_rows:
+            scratch += [pltpu.VMEM(tile_values.shape, BF16), pltpu.SemaphoreType.DMA((SLOTS // GROUP,))]
         return pl.pallas_call(
             functools.partial(product_kernel, with_rows),
             out_shape=shape((PEERS, SIDE + extra, WIDTH), BF16),
-            in_specs=[smem] * 4 + [vmem] * 5,
+            in_specs=[smem] * 4 + [hbm if with_rows else vmem, vmem, vmem],
             out_specs=vmem,
-            scratch_shapes=[pltpu.VMEM((PEERS, SIDE, width), F32)],
-            compiler_params=params,
+            scratch_shapes=scratch,
+            compiler_params=product_params if with_rows else params,
         )(place, tile_rows, tile_cols, live_count, tile_values, *parts)
 
     with jax.named_scope("gather_one"):
@@ -318,8 +352,8 @@
 
 
 def solution(mesh):
-    devices = np.asarray(mesh.devices).reshape(ZS // 2, 2, 2, 4, 4)
-    whole = ("level", "odd", "core", "x", "y")
+    devices = np.asarray(mesh.devices).reshape(QUADS, ZS // QUADS, 2, 4, 4)
+    whole = ("quad", "spot", "core", "x", "y")
     fine = Mesh(devices, whole)
     in_specs = (P(whole, None, None), P(whole), P(whole), P(whole), P(whole, None))
     return jax.shard_map(

time: 235 us -> 231 us (0.983)
  waiting for transfers between devices: 15.3 us -> 31.8 us
  blocking collectives: 134 us -> 124 us
  starting transfers between devices: 59.8 us -> 51 us
  local copies, waits for them, and re-layouts: 5.07 us -> 0.04 us
  Pallas kernels: 19.6 us -> 22.7 us
    ppermute x7 -> x8, waiting for transfers between devices: 3.74 us -> 20.3 us  [the longest x2 13.2 us: gather(): two = lax.ppermute(mine, chips, from_level(2, -2))]
    all_gather x2 -> x3, blocking collectives: 48.9 us -> 35.8 us  [the longest x2 32.2 us: gather(): mine = lax.all_gather(sent, 'quad', axis=0)]
    ppermute x7 -> x8, starting transfers between devices: 44.4 us -> 35.4 us  [the longest x2 14.9 us: gather(): return (near, lax.ppermute(near, 'core', [(0, 1), (1, 0)]))]
    unnamed x14 -> x8, local copies, waits for them, and re-layouts: 5.04 us -> 0.02 us
  transfers between devices with their start and end apart: 8 -> 9, of which waited for: 4 -> 6; matrix products, arithmetic and copies ran while one was open for 0% -> 0% of each run, Pallas kernels for 0% -> 0%
where the time goes in v3:
time: 231 us; the launch traced here: 230 us
  blocking collectives  124 us (54%)
  starting transfers between devices  51 us (22%)
  waiting for transfers between devices  31.8 us (14%)
  Pallas kernels  22.7 us (10%)
    all_to_all x2, blocking collectives, shards(): arrived = lax.all_to_all(partial_value, ('x', 'y'), 0, 0, tiled=True)  43.8 us
    all_gather x2, blocking collectives, gather(): mine = lax.all_gather(sent, 'quad', axis=0)  32.2 us
    all_to_all x1, blocking collectives, shards(): piece = jnp.sum(lax.all_to_all(spread, levels, 0, 0, tiled=True), axis=0)  18.2 us
    all_to_all x1, starting transfers between devices, shards(): pieces = jnp.sum(lax.all_to_all(part, levels, 0, 0, tiled=True), axis=0)  15.6 us
    ppermute x2, starting transfers between devices, gather(): return (near, lax.ppermute(near, 'core', [(0, 1), (1, 0)]))  14.9 us
    ppermute x2, waiting for transfers between devices, gather(): two = lax.ppermute(mine, chips, from_level(2, -2))  13.2 us
    all_to_all x1, blocking collectives, shards(): grams = lax.all_to_all(spread, plane, 0, 0, tiled=True)  13 us
    all_to_all x1, blocking collectives, shards(): piece = jnp.sum(lax.all_to_all(grams, plane, 0, 0, tiled=True), axis=0)  12.9 us
  transfers between devices with their start and end apart: 9, of which 6 were waited for; matrix products, arithmetic and copies ran while one was open for 0% of the time, Pallas kernels for 0%

profile of v3, /device:TPU:1, one launch (start us, length us, event | category | flops | bytes accessed | tf_op | source)
XLA Modules:
  0.0 230.4 jit_solution(9426456915621274077)
XLA Ops:
  0.7 3.8 %col_degree.1 = f32[16,8,128]{2,1,0:T(8,128)} custom-call(s32[32]{0:T(128)} %cols_ref.5, s32[1]{0:T(128)S(6)} %copy.6.live_ref, bf16[32,256,256]{2,1,0:T(8,128)(2,1)} %tiles_ref.5), custom_call_target="tpu_custom_call" | custom-call | tf_op jit(solution)/shard_map/col_degree/pallas_call | solution.py:257
  4.5 15.6 %all-to-all-start = ((f32[16,8,128]{2,1,0:T(8,128)}), f32[16,8,128]{2,1,0:T(8,128)S(1)}, u32[]{:S(2)}, u32[]{:S(2)}) async-start(f32[16,8,128]{2,1,0:T(8,128)} %col_degree.1), calls=%async_computation | async-start | bytes 131072 | tf_op jit(solution)/shard_map/col_degree/all_to_all | solution.py:269
  20.2 11.5 %all-to-all-done = f32[16,8,128]{2,1,0:T(8,128)S(1)} async-done(((f32[16,8,128]{2,1,0:T(8,128)}), f32[16,8,128]{2,1,0:T(8,128)S(1)}, u32[]{:S(2)}, u32[]{:S(2)}) %all-to-all-start) | async-done | bytes 65568 | tf_op jit(solution)/shard_map/col_degree/all_to_all | solution.py:269
  31.7 3.6 %all-gather = f32[16,128]{1,0:T(8,128)S(1)} all-gather(f32[8,128]{1,0:T(8,128)S(1)} %reduce_sum.27), channel_id=2, replica_groups=mesh['quad'=4,'spot'=4,'core'=2,'x'=4,'y'=4] {'core'}, dimensions={0}, use_global_device_ids=true | all-gather | bytes 12288 | tf_op jit(solution)/shard_map/col_degree/all_gather | solution.py:270
  35.3 0.7 scale.1
  36.0 16.4 %all-gather.1 = bf16[1024,128]{1,0:T(8,128)(2,1)S(1)} all-gather(bf16[256,128]{1,0:T(8,128)(2,1)S(1)} %get-tuple-element.12), channel_id=3, replica_groups=mesh['quad'=4,'spot'=4,'core'=2,'x'=4,'y'=4] {'quad'}, dimensions={0}, use_global_device_ids=true | all-gather | bytes 327680 | tf_op jit(solution)/shard_map/gather_one/all_gather | solution.py:288
  52.4 2.2 collective-permute-start.2
  54.5 3.8 %collective-permute-start.1 = (bf16[4,256,128]{2,1,0:T(8,128)(2,1)S(1)}, bf16[4,256,128]{2,1,0:T(8,128)(2,1)S(1)}, u32[]{:S(2)}, u32[]{:S(2)}) collective-permute-start(bf16[4,256,128]{2,1,0:T(8,128)(2,1)S(1)} %bitcast.7), channel_id=1, source_target_pairs={{64,0},{464,16},{96,32},{496,48},{128,64},{16,80},{160,96},{48,112... | collective-permute-start | bytes 786440 | tf_op jit(solution)/shard_map/gather_one/ppermute | solution.py:289
  58.3 4.5 %collective-permute-start = (bf16[4,256,128]{2,1,0:T(8,128)(2,1)S(1)}, bf16[4,256,128]{2,1,0:T(8,128)(2,1)S(1)}, u32[]{:S(2)}, u32[]{:S(2)}) collective-permute-start(bf16[4,256,128]{2,1,0:T(8,128)(2,1)S(1)} %bitcast.8), channel_id=1, source_target_pairs={{32,0},{48,16},{64,32},{80,48},{96,64},{112,80},{128,96},{144,112}... | collective-permute-start | bytes 786440 | tf_op jit(solution)/shard_map/gather_one/ppermute | solution.py:290
  62.8 6.0 %collective-permute-done.1 = bf16[4,256,128]{2,1,0:T(8,128)(2,1)S(1)} collective-permute-done((bf16[4,256,128]{2,1,0:T(8,128)(2,1)S(1)}, bf16[4,256,128]{2,1,0:T(8,128)(2,1)S(1)}, u32[]{:S(2)}, u32[]{:S(2)}) %collective-permute-start.1) | collective-permute-done | bytes 262176 | tf_op jit(solution)/shard_map/gather_one/ppermute | solution.py:289
  68.8 2.6 %collective-permute-done = bf16[4,256,128]{2,1,0:T(8,128)(2,1)S(1)} collective-permute-done((bf16[4,256,128]{2,1,0:T(8,128)(2,1)S(1)}, bf16[4,256,128]{2,1,0:T(8,128)(2,1)S(1)}, u32[]{:S(2)}, u32[]{:S(2)}) %collective-permute-start) | collective-permute-done | bytes 262176 | tf_op jit(solution)/shard_map/gather_one/ppermute | solution.py:290
  71.4 0.1 pad_maximum_fusion.near_ref
  71.6 6.2 %collective-permute-start.3 = (bf16[16,256,128]{2,1,0:T(8,128)(2,1)S(1)}, bf16[16,256,128]{2,1,0:T(8,128)(2,1)S(1)}, u32[]{:S(2)}, u32[]{:S(2)}) collective-permute-start(bf16[16,256,128]{2,1,0:T(8,128)(2,1)S(1)} %pad_maximum_fusion.near_ref), channel_id=1, source_target_pairs={{0,16},{16,0},{1,17},{17,1},{2,18},{18,2},{3,19},{19,3},{4,20},{20... | collective-permute-start | bytes 3145736 | tf_op jit(solution)/shard_map/gather_one/ppermute | solution.py:293
  77.7 2.3 collective-permute-done.3.far_ref
  80.0 4.0 %product_one.1 = bf16[16,272,128]{2,1,0:T(8,128)(2,1)S(1)} custom-call(s32[2]{0:T(128)S(1)} %pad_add_fusion.place_ref, s32[32]{0:T(128)S(1)} %copy-done.3, s32[32]{0:T(128)S(1)} %copy-done.2, s32[1]{0:T(128)S(6)} %copy.6.live_ref, bf16[32,256,256]{2,1,0:T(8,128)(2,1)} %tiles_ref.5, bf16[16,256,128]{2,1,0:T(8,128)(2,1)S(1)} %pad_maximum_fusion.near_ref, ...), custom_call_target="tpu_custom_call" | custom-call | tf_op jit(solution)/shard_map/product_one/pallas_call | solution.py:300
  84.1 24.7 %all_to_all.30.arrived_ref = bf16[16,272,128]{2,1,0:T(8,128)(2,1)S(1)} all-to-all(bf16[16,272,128]{2,1,0:T(8,128)(2,1)S(1)} %product_one.1), channel_id=1, replica_groups=mesh['quad'=4,'spot'=4,'core'=2,'x'=4,'y'=4] {'x','y'}, dimensions={0} | all-to-all | bytes 2228224 | tf_op jit(solution)/shard_map/reduce_one/all_to_all | solution.py:314
  108.8 0.5 middle.1
  109.2 15.8 %all-gather.2 = bf16[1024,128]{1,0:T(8,128)(2,1)S(1)} all-gather(bf16[256,128]{1,0:T(8,128)(2,1)S(1)} %get-tuple-element.14), channel_id=4, replica_groups=mesh['quad'=4,'spot'=4,'core'=2,'x'=4,'y'=4] {'quad'}, dimensions={0}, use_global_device_ids=true | all-gather | bytes 327680 | tf_op jit(solution)/shard_map/gather_two/all_gather | solution.py:288
  125.0 2.0 collective-permute-start.6
  127.1 5.8 %collective-permute-start.5 = (bf16[4,256,128]{2,1,0:T(8,128)(2,1)S(1)}, bf16[4,256,128]{2,1,0:T(8,128)(2,1)S(1)}, u32[]{:S(2)}, u32[]{:S(2)}) collective-permute-start(bf16[4,256,128]{2,1,0:T(8,128)(2,1)S(1)} %bitcast.11), channel_id=1, source_target_pairs={{64,0},{464,16},{96,32},{496,48},{128,64},{16,80},{160,96},{48,112... | collective-permute-start | bytes 786440 | tf_op jit(solution)/shard_map/gather_two/ppermute | solution.py:289
  132.9 2.2 collective-permute-start.4
  135.1 7.2 %collective-permute-done.5 = bf16[4,256,128]{2,1,0:T(8,128)(2,1)S(1)} collective-permute-done((bf16[4,256,128]{2,1,0:T(8,128)(2,1)S(1)}, bf16[4,256,128]{2,1,0:T(8,128)(2,1)S(1)}, u32[]{:S(2)}, u32[]{:S(2)}) %collective-permute-start.5) | collective-permute-done | bytes 262176 | tf_op jit(solution)/shard_map/gather_two/ppermute | solution.py:289
  142.3 0.1 pad_maximum_fusion.1.near_ref
  142.4 8.7 %collective-permute-start.7 = (bf16[16,256,128]{2,1,0:T(8,128)(2,1)S(1)}, bf16[16,256,128]{2,1,0:T(8,128)(2,1)S(1)}, u32[]{:S(2)}, u32[]{:S(2)}) collective-permute-start(bf16[16,256,128]{2,1,0:T(8,128)(2,1)S(1)} %pad_maximum_fusion.1.near_ref), channel_id=1, source_target_pairs={{0,16},{16,0},{1,17},{17,1},{2,18},{18,2},{3,19},{19,3},{4,20},{20... | collective-permute-start | bytes 3145736 | tf_op jit(solution)/shard_map/gather_two/ppermute | solution.py:293
  151.2 2.3 collective-permute-done.7.far_ref
  153.4 2.0 product_two.1
  155.5 19.1 %all_to_all.31.arrived_ref = bf16[16,256,128]{2,1,0:T(8,128)(2,1)S(1)} all-to-all(bf16[16,256,128]{2,1,0:T(8,128)(2,1)S(1)} %product_two.1), channel_id=1, replica_groups=mesh['quad'=4,'spot'=4,'core'=2,'x'=4,'y'=4] {'x','y'}, dimensions={0} | all-to-all | bytes 2097152 | tf_op jit(solution)/shard_map/reduce_two/all_to_all | solution.py:328
  174.5 0.5 last.1
  175.0 12.9 %all_to_all.32 = f32[32,8,128]{2,1,0:T(8,128)S(1)} all-to-all(f32[32,8,128]{2,1,0:T(8,128)S(1)} %get-tuple-element.17), channel_id=1, replica_groups=mesh['quad'=4,'spot'=4,'core'=2,'x'=4,'y'=4] {'core','x','y'}, dimensions={0} | all-to-all | bytes 262144 | tf_op jit(solution)/shard_map/gram/all_to_all | solution.py:339
  188.0 18.2 %all_to_all.33 = f32[16,8,128]{2,1,0:T(8,128)S(1)} all-to-all(f32[16,8,128]{2,1,0:T(8,128)S(1)} %broadcast_in_dim.4), channel_id=1, replica_groups=mesh['quad'=4,'spot'=4,'core'=2,'x'=4,'y'=4] {'quad','spot'}, dimensions={0} | all-to-all | bytes 131072 | tf_op jit(solution)/shard_map/gram/all_to_all | solution.py:341
  206.2 13.0 %all_to_all.34.grams_ref = f32[32,8,128]{2,1,0:T(8,128)S(1)} all-to-all(f32[32,8,128]{2,1,0:T(8,128)S(1)} %broadcast_in_dim.5), channel_id=1, replica_groups=mesh['quad'=4,'spot'=4,'core'=2,'x'=4,'y'=4] {'core','x','y'}, dimensions={0} | all-to-all | bytes 262144 | tf_op jit(solution)/shard_map/gram/all_to_all | solution.py:343
  219.2 11.3 %finish.1 = f32[256,128]{1,0:T(8,128)} custom-call(f32[32,8,128]{2,1,0:T(8,128)S(1)} %all_to_all.34.grams_ref, f32[256,128]{1,0:T(8,128)S(1)} %get-tuple-element.18.fresh_ref), custom_call_target="tpu_custom_call" | custom-call | tf_op jit(solution)/shard_map/finish/pallas_call | solution.py:345
  (17 shorter events, 0.2 us)
Async XLA Ops:
  0.7 34.7 %copy-start.1 = (bf16[256,128]{1,0:T(8,128)(2,1)S(1)}, bf16[256,128]{1,0:T(8,128)(2,1)}, u32[]{:S(2)}) copy-start(bf16[256,128]{1,0:T(8,128)(2,1)} %initial_ref.1) | copy-start | bytes 196612
  4.5 27.2 %all-to-all-start = ((f32[16,8,128]{2,1,0:T(8,128)}), f32[16,8,128]{2,1,0:T(8,128)S(1)}, u32[]{:S(2)}, u32[]{:S(2)}) async-start(f32[16,8,128]{2,1,0:T(8,128)} %col_degree.1), calls=%async_computation | async-start | bytes 131072 | tf_op jit(solution)/shard_map/col_degree/all_to_all | solution.py:269
  52.4 27.6 %copy-start.2 = (s32[32]{0:T(128)S(1)}, s32[32]{0:T(128)}, u32[]{:S(2)}) copy-start(s32[32]{0:T(128)} %cols_ref.5) | copy-start | bytes 388
  52.4 27.6 %copy-start.3 = (s32[32]{0:T(128)S(1)}, s32[32]{0:T(128)}, u32[]{:S(2)}) copy-start(s32[32]{0:T(128)} %rows_ref.3) | copy-start | bytes 388
  52.4 10.4 %collective-permute-start.2 = (bf16[4,256,128]{2,1,0:T(8,128)(2,1)S(1)}, bf16[4,256,128]{2,1,0:T(8,128)(2,1)S(1)}, u32[]{:S(2)}, u32[]{:S(2)}) collective-permute-start(bf16[4,256,128]{2,1,0:T(8,128)(2,1)S(1)} %bitcast.6), channel_id=1, source_target_pairs={{480,0},{496,16},{0,32},{16,48},{32,64},{48,80},{64,96},{80,112},{... | collective-permute-start | bytes 786440 | tf_op jit(solution)/shard_map/gather_one/ppermute | solution.py:291
  54.5 14.3 %collective-permute-start.1 = (bf16[4,256,128]{2,1,0:T(8,128)(2,1)S(1)}, bf16[4,256,128]{2,1,0:T(8,128)(2,1)S(1)}, u32[]{:S(2)}, u32[]{:S(2)}) collective-permute-start(bf16[4,256,128]{2,1,0:T(8,128)(2,1)S(1)} %bitcast.7), channel_id=1, source_target_pairs={{64,0},{464,16},{96,32},{496,48},{128,64},{16,80},{160,96},{48,112... | collective-permute-start | bytes 786440 | tf_op jit(solution)/shard_map/gather_one/ppermute | solution.py:289
  58.3 13.1 %collective-permute-start = (bf16[4,256,128]{2,1,0:T(8,128)(2,1)S(1)}, bf16[4,256,128]{2,1,0:T(8,128)(2,1)S(1)}, u32[]{:S(2)}, u32[]{:S(2)}) collective-permute-start(bf16[4,256,128]{2,1,0:T(8,128)(2,1)S(1)} %bitcast.8), channel_id=1, source_target_pairs={{32,0},{48,16},{64,32},{80,48},{96,64},{112,80},{128,96},{144,112}... | collective-permute-start | bytes 786440 | tf_op jit(solution)/shard_map/gather_one/ppermute | solution.py:290
  71.6 8.4 %collective-permute-start.3 = (bf16[16,256,128]{2,1,0:T(8,128)(2,1)S(1)}, bf16[16,256,128]{2,1,0:T(8,128)(2,1)S(1)}, u32[]{:S(2)}, u32[]{:S(2)}) collective-permute-start(bf16[16,256,128]{2,1,0:T(8,128)(2,1)S(1)} %pad_maximum_fusion.near_ref), channel_id=1, source_target_pairs={{0,16},{16,0},{1,17},{17,1},{2,18},{18,2},{3,19},{19,3},{4,20},{20... | collective-permute-start | bytes 3145736 | tf_op jit(solution)/shard_map/gather_one/ppermute | solution.py:293
  84.0 69.4 %copy-start = (bf16[32,256,256]{2,1,0:T(8,128)(2,1)S(1)}, bf16[32,256,256]{2,1,0:T(8,128)(2,1)}, u32[]{:S(2)}) copy-start(bf16[32,256,256]{2,1,0:T(8,128)(2,1)} %tiles_ref.5) | copy-start | bytes 12582916
  125.0 10.1 %collective-permute-start.6 = (bf16[4,256,128]{2,1,0:T(8,128)(2,1)S(1)}, bf16[4,256,128]{2,1,0:T(8,128)(2,1)S(1)}, u32[]{:S(2)}, u32[]{:S(2)}) collective-permute-start(bf16[4,256,128]{2,1,0:T(8,128)(2,1)S(1)} %bitcast.10), channel_id=1, source_target_pairs={{480,0},{496,16},{0,32},{16,48},{32,64},{48,80},{64,96},{80,112},{... | collective-permute-start | bytes 786440 | tf_op jit(solution)/shard_map/gather_two/ppermute | solution.py:291
  127.1 15.2 %collective-permute-start.5 = (bf16[4,256,128]{2,1,0:T(8,128)(2,1)S(1)}, bf16[4,256,128]{2,1,0:T(8,128)(2,1)S(1)}, u32[]{:S(2)}, u32[]{:S(2)}) collective-permute-start(bf16[4,256,128]{2,1,0:T(8,128)(2,1)S(1)} %bitcast.11), channel_id=1, source_target_pairs={{64,0},{464,16},{96,32},{496,48},{128,64},{16,80},{160,96},{48,112... | collective-permute-start | bytes 786440 | tf_op jit(solution)/shard_map/gather_two/ppermute | solution.py:289
  132.9 9.4 %collective-permute-start.4 = (bf16[4,256,128]{2,1,0:T(8,128)(2,1)S(1)}, bf16[4,256,128]{2,1,0:T(8,128)(2,1)S(1)}, u32[]{:S(2)}, u32[]{:S(2)}) collective-permute-start(bf16[4,256,128]{2,1,0:T(8,128)(2,1)S(1)} %bitcast.12), channel_id=1, source_target_pairs={{32,0},{48,16},{64,32},{80,48},{96,64},{112,80},{128,96},{144,112}... | collective-permute-start | bytes 786440 | tf_op jit(solution)/shard_map/gather_two/ppermute | solution.py:290
  142.4 11.0 %collective-permute-start.7 = (bf16[16,256,128]{2,1,0:T(8,128)(2,1)S(1)}, bf16[16,256,128]{2,1,0:T(8,128)(2,1)S(1)}, u32[]{:S(2)}, u32[]{:S(2)}) collective-permute-start(bf16[16,256,128]{2,1,0:T(8,128)(2,1)S(1)} %pad_maximum_fusion.1.near_ref), channel_id=1, source_target_pairs={{0,16},{16,0},{1,17},{17,1},{2,18},{18,2},{3,19},{19,3},{4,20},{20... | collective-permute-start | bytes 3145736 | tf_op jit(solution)/shard_map/gather_two/ppermute | solution.py:293

commit v4 on v3

--- a/solution.py
+++ b/solution.py
@@ -59,7 +59,7 @@
     return copies
 
 
-def degree_kernel(cols_ref, live_ref, tiles_ref, out_ref, held_ref, acc_ref, sems):
+def degree_kernel(cols_ref, live_ref, tiles_ref, initial_ref, out_ref, held_ref, acc_ref, sems):
     copies = tile_copies(DEGREE_PARTS, tiles_ref, held_ref, sems)
     for copy in copies:
         copy.start()
@@ -77,15 +77,21 @@
     for part, copy in enumerate(copies):
         copy.wait()
         lax.fori_loop(part * size, part * size + size, one, 0)
-    out_ref[...] = jnp.zeros_like(out_ref)
+    lane = lax.broadcasted_iota(jnp.int32, (1, WIDTH), 1)
+    last = jnp.zeros((1, WIDTH), F32)
     for block in range(2 * ZS):
         total = jnp.sum(acc_ref[block], axis=0, keepdims=True)
         at = 2 * (block % 2)
         out_ref[block // 2, at : at + 1, :] = total[:, :WIDTH]
         out_ref[block // 2, at + 1 : at + 2, :] = total[:, WIDTH:]
-
-
-def scale_kernel(place_ref, pieces_ref, initial_ref, out_ref, scale_ref):
+        last = jnp.where(lane == block, total[:, SIDE - 1 :], last)
+    row = initial_ref[SIDE - 16 :].astype(F32)[15:]
+    rest = jnp.concatenate([last, row, jnp.zeros((2, WIDTH), F32)], axis=0)
+    for peer in range(ZS):
+        out_ref[peer, 4:] = rest
+
+
+def scale_kernel(place_ref, pieces_ref, arrived_ref, initial_ref, out_ref, last_ref, scale_ref):
     both = pieces_ref[0] + pieces_ref[1]
     scale = lax.rsqrt(jnp.where(place_ref[0] == 0, both[0:2], both[2:4]))
     scale_ref[...] = scale
@@ -93,6 +99,11 @@
         rows = slice(half * WIDTH, (half + 1) * WIDTH)
         column = to_column(scale[half : half + 1])
         out_ref[rows] = (column * initial_ref[rows].astype(F32)).astype(BF16)
+    level = lax.broadcasted_iota(jnp.int32, (ZS, WIDTH), 0)
+    lane = lax.broadcasted_iota(jnp.int32, (ZS, WIDTH), 1)
+    picked = jnp.where(lane == 2 * level + place_ref[0], jnp.broadcast_to(both[4:5], (ZS, WIDTH)), 0.0)
+    degree = jnp.sum(picked, axis=1, keepdims=True)
+    last_ref[...] = (lax.rsqrt(degree) * arrived_ref[:, 5, :]).astype(BF16)
 
 
 def product_kernel(with_rows, place_ref, rows_ref, cols_ref, live_ref, tiles_ref, near_ref, far_ref, out_ref, acc_ref, *held):
@@ -108,7 +119,10 @@
     def product(slot):
         col = cols_ref[slot]
         core, level = lax.rem(col, 2), lax.div(col, 2)
-        at = QUADS * lax.rem(level + QUADS - place_ref[1], QUADS) + lax.div(level, QUADS)
+        if with_rows:
+            at = level
+        else:
+            at = QUADS * lax.rem(level + QUADS - place_ref[1], QUADS) + lax.div(level, QUADS)
         block = jnp.where(core == place_ref[0], near_ref[at], far_ref[at])
         if with_rows:
             block = jnp.concatenate([block, jnp.ones((SIDE, WIDTH), BF16)], axis=1)
@@ -200,14 +214,21 @@
             unit = jnp.where(lane == at + i, 1.0, 0.0)
             rows.append(jnp.where(inside, unit, jnp.broadcast_to(panel[i : i + 1], (8, WIDTH))))
         inverse, lower = [], {}
-        for p in range(8):
-            inverse.append(1.0 / left[p, p])
-            for i in range(p + 1, 8):
-                lower[i, p] = left[i, p] * inverse[p]
-            for i in range(p + 1, 8):
-                for j in range(p + 1, i + 1):
-                    left[i, j] = left[i, j] - lower[i, p] * left[j, p]
-                rows[i] = rows[i] - lower[i, p] * rows[p]
+        for p in range(0, 8, 2):
+            a, b, c = left[p, p], left[p + 1, p], left[p + 1, p + 1]
+            scale = 1.0 / (a * c - b * b)
+            corner, cross, pivot = c * scale, b * scale, a * scale
+            inverse += [1.0 / a, pivot]
+            lower[p + 1, p] = b * inverse[p]
+            left[p + 1, p + 1] = c - b * lower[p + 1, p]
+            for i in range(p + 2, 8):
+                first = left[i, p] * corner - left[i, p + 1] * cross
+                second = left[i, p + 1] * pivot - left[i, p] * cross
+                lower[i, p], lower[i, p + 1] = left[i, p] * inverse[p], second
+                for j in range(p + 2, i + 1):
+                    left[i, j] = left[i, j] - (first * left[j, p] + second * left[j, p + 1])
+                rows[i] = rows[i] - (first * rows[p] + second * rows[p + 1])
+            rows[p + 1] = rows[p + 1] - lower[p + 1, p] * rows[p]
         total = jnp.zeros((8, WIDTH), F32)
         for i in range(8):
             total = jnp.where(row == i, rows[i] * lax.rsqrt(left[i, i]), total)
@@ -252,12 +273,13 @@
     place = jnp.stack([core, lax.axis_index("spot")]).astype(jnp.int32)
     levels = ("quad", "spot")
     plane = ("core", "x", "y")
+    swap = [(0, 1), (1, 0)]
 
     with jax.named_scope("col_degree"):
         part = pl.pallas_call(
             degree_kernel,
             out_shape=shape((ZS, 8, WIDTH), F32),
-            in_specs=[smem, smem, hbm],
+            in_specs=[smem, smem, hbm, vmem],
             out_specs=vmem,
             scratch_shapes=[
                 pltpu.VMEM(tile_values.shape, BF16),
@@ -265,17 +287,21 @@
                 pltpu.SemaphoreType.DMA((DEGREE_PARTS,)),
             ],
             compiler_params=degree_params,
-        )(tile_cols, live_count, tile_values)
-        pieces = jnp.sum(lax.all_to_all(part, levels, 0, 0, tiled=True), axis=0)
-        pieces = lax.all_gather(pieces, "core", axis=0)
+        )(tile_cols, live_count, tile_values, initial)
+        degrees = lax.all_to_all(part, levels, 0, 0, tiled=True)
+        pieces = lax.all_gather(jnp.sum(degrees, axis=0), "core", axis=0)
     with jax.named_scope("scale"):
-        sent, col_scale = pl.pallas_call(
+        sent, last, col_scale = pl.pallas_call(
             scale_kernel,
-            out_shape=(shape((SIDE, WIDTH), BF16), shape((2, WIDTH), F32)),
-            in_specs=[smem, vmem, vmem],
-            out_specs=(vmem, vmem),
+            out_shape=(
+                shape((SIDE, WIDTH), BF16),
+                shape((ZS, WIDTH), BF16),
+                shape((2, WIDTH), F32),
+            ),
+            in_specs=[smem] + [vmem] * 3,
+            out_specs=(vmem,) * 3,
             compiler_params=params,
-        )(place, pieces, initial)
+        )(place, pieces, degrees, initial)
 
     def from_level(first, second):
         steps = (first, second)
@@ -290,7 +316,7 @@
         one = lax.ppermute(mine, chips, from_level(1, 1))
         three = lax.ppermute(mine, chips, from_level(-1, -1))
         near = jnp.concatenate([mine, one, two, three], axis=0)
-        return near, lax.ppermute(near, "core", [(0, 1), (1, 0)])
+        return near, lax.ppermute(near, "core", swap)
 
     def product(with_rows, parts):
         extra, width = (EXTRA, 2 * WIDTH) if with_rows else (0, WIDTH)
@@ -307,7 +333,9 @@
         )(place, tile_rows, tile_cols, live_count, tile_values, *parts)
 
     with jax.named_scope("gather_one"):
-        parts = gather(sent)
+        near = lax.all_gather(sent[: SIDE - 1], levels, axis=0)
+        near = jnp.concatenate([near, last[:, None]], axis=1)
+        parts = near, lax.ppermute(near, "core", swap)
     with jax.named_scope("product_one"):
         partial_value = product(True, parts)
     with jax.named_scope("reduce_one"):

time: 231 us -> 224 us (0.970)
  blocking collectives: 124 us -> 133 us
  waiting for transfers between devices: 31.8 us -> 22.9 us
  starting transfers between devices: 51 us -> 43 us
    all_gather x1 -> x2, blocking collectives: 3.6 us -> 30.3 us  [the longest x1 26.6 us: shards(): near = lax.all_gather(sent[:SIDE - 1], levels, axis=0)]
    all_gather x2 -> x1, blocking collectives: 32.2 us -> 16.6 us  [gather(): mine = lax.all_gather(sent, 'quad', axis=0)]
    ppermute x2 -> x1, starting transfers between devices: 9.62 us -> 1.92 us  [gather(): two = lax.ppermute(mine, chips, from_level(2, -2))]
    ppermute x2 -> x1, waiting for transfers between devices: 13.2 us -> 6.93 us  [gather(): two = lax.ppermute(mine, chips, from_level(2, -2))]
    ppermute x2, starting transfers between devices: 14.9 us -> 18.7 us  [the longest x1 9.6 us: gather(): return (near, lax.ppermute(near, 'core', swap))]
    ppermute x2 -> x1, waiting for transfers between devices: 2.59 us -> 0.01 us  [gather(): one = lax.ppermute(mine, chips, from_level(1, 1))]
    ppermute x2 -> x1, starting transfers between devices: 6.69 us -> 4.57 us  [gather(): one = lax.ppermute(mine, chips, from_level(1, 1))]
  transfers between devices with their start and end apart: 9 -> 6, of which waited for: 6 -> 4; matrix products, arithmetic and copies ran while one was open for 0% -> 0% of each run, Pallas kernels for 0% -> 0%
where the time goes in v4:
time: 224 us; the launch traced here: 223 us
  blocking collectives  133 us (59%)
  starting transfers between devices  43 us (19%)
  waiting for transfers between devices  22.9 us (10%)
  Pallas kernels  22.6 us (10%)
    all_to_all x2, blocking collectives, shards(): arrived = lax.all_to_all(partial_value, ('x', 'y'), 0, 0, tiled=True)  42.7 us
    all_gather x1, blocking collectives, shards(): near = lax.all_gather(sent[:SIDE - 1], levels, axis=0)  26.6 us
    all_to_all x1, blocking collectives, shards(): piece = jnp.sum(lax.all_to_all(spread, levels, 0, 0, tiled=True), axis=0)  17.8 us
    all_gather x1, blocking collectives, gather(): mine = lax.all_gather(sent, 'quad', axis=0)  16.6 us
    all_to_all x1, starting transfers between devices, shards(): degrees = lax.all_to_all(part, levels, 0, 0, tiled=True)  15.9 us
    all_to_all x1, blocking collectives, shards(): grams = lax.all_to_all(spread, plane, 0, 0, tiled=True)  13 us
    all_to_all x1, blocking collectives, shards(): piece = jnp.sum(lax.all_to_all(grams, plane, 0, 0, tiled=True), axis=0)  12.9 us
    all_to_all x1, waiting for transfers between devices, shards(): degrees = lax.all_to_all(part, levels, 0, 0, tiled=True)  11.5 us
  transfers between devices with their start and end apart: 6, of which 4 were waited for; matrix products, arithmetic and copies ran while one was open for 0% of the time, Pallas kernels for 0%

profile of v4, /device:TPU:1, one launch (start us, length us, event | category | flops | bytes accessed | tf_op | source)
XLA Modules:
  0.0 223.2 jit_solution(12221385877382354389)
XLA Ops:
  0.7 3.9 %col_degree.1 = f32[16,8,128]{2,1,0:T(8,128)} custom-call(s32[32]{0:T(128)} %cols_ref.5, s32[1]{0:T(128)S(6)} %copy.9.live_ref, bf16[32,256,256]{2,1,0:T(8,128)(2,1)} %tiles_ref.5, bf16[256,128]{1,0:T(8,128)(2,1)} %initial_ref.3), custom_call_target="tpu_custom_call" | custom-call | tf_op jit(solution)/shard_map/col_degree/pallas_call | solution.py:279
  4.5 0.0 copy-start.2
  4.5 0.0 copy-start.3
  4.6 15.9 %all-to-all-start = ((f32[16,8,128]{2,1,0:T(8,128)}), f32[16,8,128]{2,1,0:T(8,128)S(1)}, u32[]{:S(2)}, u32[]{:S(2)}) async-start(f32[16,8,128]{2,1,0:T(8,128)} %col_degree.1), calls=%async_computation | async-start | bytes 131072 | tf_op jit(solution)/shard_map/col_degree/all_to_all | solution.py:291
  20.5 0.1 pad_add_fusion.place_ref
  20.6 11.5 %all-to-all-done.arrived_ref = f32[16,8,128]{2,1,0:T(8,128)S(1)} async-done(((f32[16,8,128]{2,1,0:T(8,128)}), f32[16,8,128]{2,1,0:T(8,128)S(1)}, u32[]{:S(2)}, u32[]{:S(2)}) %all-to-all-start) | async-done | bytes 65568 | tf_op jit(solution)/shard_map/col_degree/all_to_all | solution.py:291
  32.1 3.7 %all-gather = f32[16,128]{1,0:T(8,128)S(1)} all-gather(f32[8,128]{1,0:T(8,128)S(1)} %reduce_sum.27), channel_id=2, replica_groups=mesh['quad'=4,'spot'=4,'core'=2,'x'=4,'y'=4] {'core'}, dimensions={0}, use_global_device_ids=true | all-gather | bytes 12288 | tf_op jit(solution)/shard_map/col_degree/all_gather | solution.py:292
  35.8 0.7 scale.1
  36.5 26.6 %all-gather.3 = bf16[16,255,128]{2,1,0:T(8,128)(2,1)S(1)} all-gather(bf16[1,255,128]{2,1,0:T(8,128)(2,1)S(1)} %slice_bitcast_fusion), channel_id=3, replica_groups=mesh['quad'=4,'spot'=4,'core'=2,'x'=4,'y'=4] {'quad','spot'}, dimensions={0}, use_global_device_ids=true | all-gather | bytes 1109760 | tf_op jit(solution)/shard_map/gather_one/all_gather | solution.py:336
  63.1 0.1 pad_maximum_fusion.near_ref
  63.2 9.1 %collective-permute-start = (bf16[16,256,128]{2,1,0:T(8,128)(2,1)S(1)}, bf16[16,256,128]{2,1,0:T(8,128)(2,1)S(1)}, u32[]{:S(2)}, u32[]{:S(2)}) collective-permute-start(bf16[16,256,128]{2,1,0:T(8,128)(2,1)S(1)} %pad_maximum_fusion.near_ref), channel_id=1, source_target_pairs={{0,16},{16,0},{1,17},{17,1},{2,18},{18,2},{3,19},{19,3},{4,20},{20... | collective-permute-start | bytes 3145736 | tf_op jit(solution)/shard_map/gather_one/ppermute | solution.py:338
  72.3 2.3 %collective-permute-done.far_ref = bf16[16,256,128]{2,1,0:T(8,128)(2,1)S(1)} collective-permute-done((bf16[16,256,128]{2,1,0:T(8,128)(2,1)S(1)}, bf16[16,256,128]{2,1,0:T(8,128)(2,1)S(1)}, u32[]{:S(2)}, u32[]{:S(2)}) %collective-permute-start) | collective-permute-done | bytes 1048608 | tf_op jit(solution)/shard_map/gather_one/ppermute | solution.py:338
  74.6 4.1 %product_one.1 = bf16[16,272,128]{2,1,0:T(8,128)(2,1)S(1)} custom-call(s32[2]{0:T(128)S(1)} %pad_add_fusion.place_ref, s32[32]{0:T(128)S(1)} %copy-done.3, s32[32]{0:T(128)S(1)} %copy-done.2, s32[1]{0:T(128)S(6)} %copy.9.live_ref, bf16[32,256,256]{2,1,0:T(8,128)(2,1)} %tiles_ref.5, bf16[16,256,128]{2,1,0:T(8,128)(2,1)S(1)} %pad_maximum_fusion.near_ref, ...), custom_call_target="tpu_custom_call" | custom-call | tf_op jit(solution)/shard_map/product_one/pallas_call | solution.py:326
  78.7 0.0 copy-start
  78.7 23.8 %all_to_all.30.arrived_ref = bf16[16,272,128]{2,1,0:T(8,128)(2,1)S(1)} all-to-all(bf16[16,272,128]{2,1,0:T(8,128)(2,1)S(1)} %product_one.1), channel_id=1, replica_groups=mesh['quad'=4,'spot'=4,'core'=2,'x'=4,'y'=4] {'x','y'}, dimensions={0} | all-to-all | bytes 2228224 | tf_op jit(solution)/shard_map/reduce_one/all_to_all | solution.py:342
  102.6 0.5 middle.1
  103.0 16.6 %all-gather.2 = bf16[1024,128]{1,0:T(8,128)(2,1)S(1)} all-gather(bf16[256,128]{1,0:T(8,128)(2,1)S(1)} %get-tuple-element.16), channel_id=4, replica_groups=mesh['quad'=4,'spot'=4,'core'=2,'x'=4,'y'=4] {'quad'}, dimensions={0}, use_global_device_ids=true | all-gather | bytes 327680 | tf_op jit(solution)/shard_map/gather_two/all_gather | solution.py:314
  119.7 1.9 collective-permute-start.3
  121.6 1.9 collective-permute-start.2
  123.5 4.6 %collective-permute-start.1 = (bf16[4,256,128]{2,1,0:T(8,128)(2,1)S(1)}, bf16[4,256,128]{2,1,0:T(8,128)(2,1)S(1)}, u32[]{:S(2)}, u32[]{:S(2)}) collective-permute-start(bf16[4,256,128]{2,1,0:T(8,128)(2,1)S(1)} %bitcast.11), channel_id=1, source_target_pairs={{32,0},{48,16},{64,32},{80,48},{96,64},{112,80},{128,96},{144,112}... | collective-permute-start | bytes 786440 | tf_op jit(solution)/shard_map/gather_two/ppermute | solution.py:316
  128.1 0.0 collective-permute-done.3
  128.1 6.9 %collective-permute-done.2 = bf16[4,256,128]{2,1,0:T(8,128)(2,1)S(1)} collective-permute-done((bf16[4,256,128]{2,1,0:T(8,128)(2,1)S(1)}, bf16[4,256,128]{2,1,0:T(8,128)(2,1)S(1)}, u32[]{:S(2)}, u32[]{:S(2)}) %collective-permute-start.2) | collective-permute-done | bytes 262176 | tf_op jit(solution)/shard_map/gather_two/ppermute | solution.py:315
  135.0 0.1 pad_maximum_fusion.1.near_ref
  135.2 9.6 %collective-permute-start.4 = (bf16[16,256,128]{2,1,0:T(8,128)(2,1)S(1)}, bf16[16,256,128]{2,1,0:T(8,128)(2,1)S(1)}, u32[]{:S(2)}, u32[]{:S(2)}) collective-permute-start(bf16[16,256,128]{2,1,0:T(8,128)(2,1)S(1)} %pad_maximum_fusion.1.near_ref), channel_id=1, source_target_pairs={{0,16},{16,0},{1,17},{17,1},{2,18},{18,2},{3,19},{19,3},{4,20},{20... | collective-permute-start | bytes 3145736 | tf_op jit(solution)/shard_map/gather_two/ppermute | solution.py:319
  144.8 2.3 %collective-permute-done.4.far_ref = bf16[16,256,128]{2,1,0:T(8,128)(2,1)S(1)} collective-permute-done((bf16[16,256,128]{2,1,0:T(8,128)(2,1)S(1)}, bf16[16,256,128]{2,1,0:T(8,128)(2,1)S(1)}, u32[]{:S(2)}, u32[]{:S(2)}) %collective-permute-start.4) | collective-permute-done | bytes 1048608 | tf_op jit(solution)/shard_map/gather_two/ppermute | solution.py:319
  147.0 2.0 product_two.1
  149.1 18.9 %all_to_all.31.arrived_ref = bf16[16,256,128]{2,1,0:T(8,128)(2,1)S(1)} all-to-all(bf16[16,256,128]{2,1,0:T(8,128)(2,1)S(1)} %product_two.1), channel_id=1, replica_groups=mesh['quad'=4,'spot'=4,'core'=2,'x'=4,'y'=4] {'x','y'}, dimensions={0} | all-to-all | bytes 2097152 | tf_op jit(solution)/shard_map/reduce_two/all_to_all | solution.py:356
  167.9 0.5 last.1
  168.4 12.9 %all_to_all.32 = f32[32,8,128]{2,1,0:T(8,128)S(1)} all-to-all(f32[32,8,128]{2,1,0:T(8,128)S(1)} %get-tuple-element.19), channel_id=1, replica_groups=mesh['quad'=4,'spot'=4,'core'=2,'x'=4,'y'=4] {'core','x','y'}, dimensions={0} | all-to-all | bytes 262144 | tf_op jit(solution)/shard_map/gram/all_to_all | solution.py:367
  181.3 17.8 %all_to_all.33 = f32[16,8,128]{2,1,0:T(8,128)S(1)} all-to-all(f32[16,8,128]{2,1,0:T(8,128)S(1)} %broadcast_in_dim.7), channel_id=1, replica_groups=mesh['quad'=4,'spot'=4,'core'=2,'x'=4,'y'=4] {'quad','spot'}, dimensions={0} | all-to-all | bytes 131072 | tf_op jit(solution)/shard_map/gram/all_to_all | solution.py:369
  199.2 13.0 %all_to_all.34.grams_ref = f32[32,8,128]{2,1,0:T(8,128)S(1)} all-to-all(f32[32,8,128]{2,1,0:T(8,128)S(1)} %broadcast_in_dim.8), channel_id=1, replica_groups=mesh['quad'=4,'spot'=4,'core'=2,'x'=4,'y'=4] {'core','x','y'}, dimensions={0} | all-to-all | bytes 262144 | tf_op jit(solution)/shard_map/gram/all_to_all | solution.py:371
  212.2 11.0 %finish.1 = f32[256,128]{1,0:T(8,128)} custom-call(f32[32,8,128]{2,1,0:T(8,128)S(1)} %all_to_all.34.grams_ref, f32[256,128]{1,0:T(8,128)S(1)} %get-tuple-element.20.fresh_ref), custom_call_target="tpu_custom_call" | custom-call | tf_op jit(solution)/shard_map/finish/pallas_call | solution.py:373
  (13 shorter events, 0.1 us)
Async XLA Ops:
  0.7 35.2 %copy-start.1 = (bf16[256,128]{1,0:T(8,128)(2,1)S(1)}, bf16[256,128]{1,0:T(8,128)(2,1)}, u32[]{:S(2)}) copy-start(bf16[256,128]{1,0:T(8,128)(2,1)} %initial_ref.3) | copy-start | bytes 196612
  4.5 70.1 %copy-start.2 = (s32[32]{0:T(128)S(1)}, s32[32]{0:T(128)}, u32[]{:S(2)}) copy-start(s32[32]{0:T(128)} %cols_ref.5) | copy-start | bytes 388
  4.5 70.0 %copy-start.3 = (s32[32]{0:T(128)S(1)}, s32[32]{0:T(128)}, u32[]{:S(2)}) copy-start(s32[32]{0:T(128)} %rows_ref.3) | copy-start | bytes 388
  4.6 27.5 %all-to-all-start = ((f32[16,8,128]{2,1,0:T(8,128)}), f32[16,8,128]{2,1,0:T(8,128)S(1)}, u32[]{:S(2)}, u32[]{:S(2)}) async-start(f32[16,8,128]{2,1,0:T(8,128)} %col_degree.1), calls=%async_computation | async-start | bytes 131072 | tf_op jit(solution)/shard_map/col_degree/all_to_all | solution.py:291
  63.2 11.3 %collective-permute-start = (bf16[16,256,128]{2,1,0:T(8,128)(2,1)S(1)}, bf16[16,256,128]{2,1,0:T(8,128)(2,1)S(1)}, u32[]{:S(2)}, u32[]{:S(2)}) collective-permute-start(bf16[16,256,128]{2,1,0:T(8,128)(2,1)S(1)} %pad_maximum_fusion.near_ref), channel_id=1, source_target_pairs={{0,16},{16,0},{1,17},{17,1},{2,18},{18,2},{3,19},{19,3},{4,20},{20... | collective-permute-start | bytes 3145736 | tf_op jit(solution)/shard_map/gather_one/ppermute | solution.py:338
  78.7 68.3 %copy-start = (bf16[32,256,256]{2,1,0:T(8,128)(2,1)S(1)}, bf16[32,256,256]{2,1,0:T(8,128)(2,1)}, u32[]{:S(2)}) copy-start(bf16[32,256,256]{2,1,0:T(8,128)(2,1)} %tiles_ref.5) | copy-start | bytes 12582916
  119.7 8.4 %collective-permute-start.3 = (bf16[4,256,128]{2,1,0:T(8,128)(2,1)S(1)}, bf16[4,256,128]{2,1,0:T(8,128)(2,1)S(1)}, u32[]{:S(2)}, u32[]{:S(2)}) collective-permute-start(bf16[4,256,128]{2,1,0:T(8,128)(2,1)S(1)} %bitcast.9), channel_id=1, source_target_pairs={{480,0},{496,16},{0,32},{16,48},{32,64},{48,80},{64,96},{80,112},{... | collective-permute-start | bytes 786440 | tf_op jit(solution)/shard_map/gather_two/ppermute | solution.py:317
  121.6 13.4 %collective-permute-start.2 = (bf16[4,256,128]{2,1,0:T(8,128)(2,1)S(1)}, bf16[4,256,128]{2,1,0:T(8,128)(2,1)S(1)}, u32[]{:S(2)}, u32[]{:S(2)}) collective-permute-start(bf16[4,256,128]{2,1,0:T(8,128)(2,1)S(1)} %bitcast.10), channel_id=1, source_target_pairs={{64,0},{464,16},{96,32},{496,48},{128,64},{16,80},{160,96},{48,112... | collective-permute-start | bytes 786440 | tf_op jit(solution)/shard_map/gather_two/ppermute | solution.py:315
  123.5 11.5 %collective-permute-start.1 = (bf16[4,256,128]{2,1,0:T(8,128)(2,1)S(1)}, bf16[4,256,128]{2,1,0:T(8,128)(2,1)S(1)}, u32[]{:S(2)}, u32[]{:S(2)}) collective-permute-start(bf16[4,256,128]{2,1,0:T(8,128)(2,1)S(1)} %bitcast.11), channel_id=1, source_target_pairs={{32,0},{48,16},{64,32},{80,48},{96,64},{112,80},{128,96},{144,112}... | collective-permute-start | bytes 786440 | tf_op jit(solution)/shard_map/gather_two/ppermute | solution.py:316
  135.2 11.9 %collective-permute-start.4 = (bf16[16,256,128]{2,1,0:T(8,128)(2,1)S(1)}, bf16[16,256,128]{2,1,0:T(8,128)(2,1)S(1)}, u32[]{:S(2)}, u32[]{:S(2)}) collective-permute-start(bf16[16,256,128]{2,1,0:T(8,128)(2,1)S(1)} %pad_maximum_fusion.1.near_ref), channel_id=1, source_target_pairs={{0,16},{16,0},{1,17},{17,1},{2,18},{18,2},{3,19},{19,3},{4,20},{20... | collective-permute-start | bytes 3145736 | tf_op jit(solution)/shard_map/gather_two/ppermute | solution.py:319

commit v5 on v4

--- a/solution.py
+++ b/solution.py
@@ -91,8 +91,10 @@
         out_ref[peer, 4:] = rest
 
 
-def scale_kernel(place_ref, pieces_ref, arrived_ref, initial_ref, out_ref, last_ref, scale_ref):
-    both = pieces_ref[0] + pieces_ref[1]
+def scale_kernel(place_ref, degrees_ref, initial_ref, out_ref, last_ref, scale_ref):
+    both = degrees_ref[0, 0] + degrees_ref[1, 0]
+    for level in range(1, ZS):
+        both += degrees_ref[0, level] + degrees_ref[1, level]
     scale = lax.rsqrt(jnp.where(place_ref[0] == 0, both[0:2], both[2:4]))
     scale_ref[...] = scale
     for half in range(2):
@@ -101,9 +103,11 @@
         out_ref[rows] = (column * initial_ref[rows].astype(F32)).astype(BF16)
     level = lax.broadcasted_iota(jnp.int32, (ZS, WIDTH), 0)
     lane = lax.broadcasted_iota(jnp.int32, (ZS, WIDTH), 1)
-    picked = jnp.where(lane == 2 * level + place_ref[0], jnp.broadcast_to(both[4:5], (ZS, WIDTH)), 0.0)
+    core = lax.rem(lax.div(level, QUADS) + place_ref[2], 2)
+    picked = jnp.where(lane == 2 * level + core, jnp.broadcast_to(both[4:5], (ZS, WIDTH)), 0.0)
     degree = jnp.sum(picked, axis=1, keepdims=True)
-    last_ref[...] = (lax.rsqrt(degree) * arrived_ref[:, 5, :]).astype(BF16)
+    row = jnp.where(core == 0, degrees_ref[0, :, 5, :], degrees_ref[1, :, 5, :])
+    last_ref[...] = (lax.rsqrt(degree) * row).astype(BF16)
 
 
 def product_kernel(with_rows, place_ref, rows_ref, cols_ref, live_ref, tiles_ref, near_ref, far_ref, out_ref, acc_ref, *held):
@@ -120,10 +124,11 @@
         col = cols_ref[slot]
         core, level = lax.rem(col, 2), lax.div(col, 2)
         if with_rows:
-            at = level
+            at, same = level, lax.rem(core + lax.div(level, QUADS), 2) == place_ref[2]
         else:
             at = QUADS * lax.rem(level + QUADS - place_ref[1], QUADS) + lax.div(level, QUADS)
-        block = jnp.where(core == place_ref[0], near_ref[at], far_ref[at])
+            same = core == place_ref[0]
+        block = jnp.where(same, near_ref[at], far_ref[at])
         if with_rows:
             block = jnp.concatenate([block, jnp.ones((SIDE, WIDTH), BF16)], axis=1)
         block = jnp.where(slot < live, block, jnp.zeros_like(block))
@@ -270,7 +275,9 @@
 
 def shards(tile_values, tile_rows, tile_cols, live_count, initial):
     core = lax.axis_index("core")
-    place = jnp.stack([core, lax.axis_index("spot")]).astype(jnp.int32)
+    group = lax.rem(core + lax.axis_index("quad"), 2)
+    place = jnp.stack([core, lax.axis_index("spot"), group]).astype(jnp.int32)
+    groups = [[2 * z + (at + z // QUADS) % 2 for z in range(ZS)] for at in range(2)]
     levels = ("quad", "spot")
     plane = ("core", "x", "y")
     swap = [(0, 1), (1, 0)]
@@ -289,7 +296,7 @@
             compiler_params=degree_params,
         )(tile_cols, live_count, tile_values, initial)
         degrees = lax.all_to_all(part, levels, 0, 0, tiled=True)
-        pieces = lax.all_gather(jnp.sum(degrees, axis=0), "core", axis=0)
+        degrees = lax.all_gather(degrees, "core", axis=0)
     with jax.named_scope("scale"):
         sent, last, col_scale = pl.pallas_call(
             scale_kernel,
@@ -298,10 +305,10 @@
                 shape((ZS, WIDTH), BF16),
                 shape((2, WIDTH), F32),
             ),
-            in_specs=[smem] + [vmem] * 3,
+            in_specs=[smem] + [vmem] * 2,
             out_specs=(vmem,) * 3,
             compiler_params=params,
-        )(place, pieces, degrees, initial)
+        )(place, degrees, initial)
 
     def from_level(first, second):
         steps = (first, second)
@@ -333,7 +340,7 @@
         )(place, tile_rows, tile_cols, live_count, tile_values, *parts)
 
     with jax.named_scope("gather_one"):
-        near = lax.all_gather(sent[: SIDE - 1], levels, axis=0)
+        near = lax.all_gather(sent[: SIDE - 1], levels + ("core",), axis=0, axis_index_groups=groups)
         near = jnp.concatenate([near, last[:, None]], axis=1)
         parts = near, lax.ppermute(near, "core", swap)
     with jax.named_scope("product_one"):

time: 224 us -> 222 us (level)
  starting transfers between devices: 43 us -> 35 us
  blocking collectives: 133 us -> 140 us
    ppermute x1, starting transfers between devices: 9.07 us -> 2.08 us  [shards(): parts = (near, lax.ppermute(near, 'core', swap))]
    all_gather x2, blocking collectives: 30.3 us -> 35.3 us  [the longest x1 31.7 us: shards(): lax.all_gather(sent[:SIDE - 1], levels + ('core',), axis=0, axis_index_gr...]
where the time goes in v5:
time: 222 us
  blocking collectives  140 us (63%)
  starting transfers between devices  35 us (16%)
  waiting for transfers between devices  23.2 us (10%)
  Pallas kernels  22.4 us (10%)
    all_to_all x2, blocking collectives, shards(): arrived = lax.all_to_all(partial_value, ('x', 'y'), 0, 0, tiled=True)  43.5 us
    all_gather x1, blocking collectives, shards(): lax.all_gather(sent[:SIDE - 1], levels + ('core',), axis=0, axis_index_gr...  31.7 us
    all_to_all x1, blocking collectives, shards(): piece = jnp.sum(lax.all_to_all(spread, levels, 0, 0, tiled=True), axis=0)  17.8 us
    all_gather x1, blocking collectives, gather(): mine = lax.all_gather(sent, 'quad', axis=0)  17 us
    all_to_all x1, starting transfers between devices, shards(): degrees = lax.all_to_all(part, levels, 0, 0, tiled=True)  15.8 us
    all_to_all x1, blocking collectives, shards(): grams = lax.all_to_all(spread, plane, 0, 0, tiled=True)  13 us
    all_to_all x1, blocking collectives, shards(): piece = jnp.sum(lax.all_to_all(grams, plane, 0, 0, tiled=True), axis=0)  12.9 us
    all_to_all x1, waiting for transfers between devices, shards(): degrees = lax.all_to_all(part, levels, 0, 0, tiled=True)  11.5 us
  transfers between devices with their start and end apart: 6, of which 4 were waited for; matrix products, arithmetic and copies ran while one was open for 0% of the time, Pallas kernels for 0%

profile of v5, /device:TPU:1, one launch (start us, length us, event | category | flops | bytes accessed | tf_op | source)
XLA Modules:
  0.0 221.6 jit_solution(9662444617927419217)
XLA Ops:
  0.7 3.9 %col_degree.1 = f32[16,8,128]{2,1,0:T(8,128)} custom-call(s32[32]{0:T(128)} %cols_ref.5, s32[1]{0:T(128)S(6)} %copy.9.live_ref, bf16[32,256,256]{2,1,0:T(8,128)(2,1)} %tiles_ref.5, bf16[256,128]{1,0:T(8,128)(2,1)} %initial_ref.3), custom_call_target="tpu_custom_call" | custom-call | tf_op jit(solution)/shard_map/col_degree/pallas_call | solution.py:286
  4.5 0.0 copy-start.2
  4.5 0.0 copy-start.3
  4.6 15.8 %all-to-all-start = ((f32[16,8,128]{2,1,0:T(8,128)}), f32[16,8,128]{2,1,0:T(8,128)S(1)}, u32[]{:S(2)}, u32[]{:S(2)}) async-start(f32[16,8,128]{2,1,0:T(8,128)} %col_degree.1), calls=%async_computation | async-start | bytes 131072 | tf_op jit(solution)/shard_map/col_degree/all_to_all | solution.py:298
  20.3 0.1 pad_add_fusion.place_ref
  20.4 11.5 %all-to-all-done = f32[16,8,128]{2,1,0:T(8,128)S(1)} async-done(((f32[16,8,128]{2,1,0:T(8,128)}), f32[16,8,128]{2,1,0:T(8,128)S(1)}, u32[]{:S(2)}, u32[]{:S(2)}) %all-to-all-start) | async-done | bytes 65568 | tf_op jit(solution)/shard_map/col_degree/all_to_all | solution.py:298
  31.9 3.6 %all-gather = f32[32,8,128]{2,1,0:T(8,128)S(1)} all-gather(f32[16,8,128]{2,1,0:T(8,128)S(1)} %all-to-all-done), channel_id=2, replica_groups=mesh['quad'=4,'spot'=4,'core'=2,'x'=4,'y'=4] {'core'}, dimensions={0}, use_global_device_ids=true | all-gather | bytes 196608 | tf_op jit(solution)/shard_map/col_degree/all_gather | solution.py:299
  35.5 0.7 scale.1
  36.2 31.7 %all-gather.3 = bf16[16,255,128]{2,1,0:T(8,128)(2,1)S(1)} all-gather(bf16[1,255,128]{2,1,0:T(8,128)(2,1)S(1)} %slice_bitcast_fusion), channel_id=3, replica_groups={{0,32,64,96,144,176,208,240,256,288,320,352,400,432,464,496},{16,48,80,..., dimensions={0}, use_global_device_ids=true | all-gather | bytes 1109760 | tf_op jit(solution)/shard_map/gather_one/all_gather | solution.py:343
  67.9 0.1 pad_maximum_fusion.near_ref
  68.1 2.1 collective-permute-start
  70.1 2.5 %collective-permute-done.far_ref = bf16[16,256,128]{2,1,0:T(8,128)(2,1)S(1)} collective-permute-done((bf16[16,256,128]{2,1,0:T(8,128)(2,1)S(1)}, bf16[16,256,128]{2,1,0:T(8,128)(2,1)S(1)}, u32[]{:S(2)}, u32[]{:S(2)}) %collective-permute-start) | collective-permute-done | bytes 1048608 | tf_op jit(solution)/shard_map/gather_one/ppermute | solution.py:345
  72.6 4.0 %product_one.1 = bf16[16,272,128]{2,1,0:T(8,128)(2,1)S(1)} custom-call(s32[3]{0:T(128)S(1)} %pad_add_fusion.place_ref, s32[32]{0:T(128)S(1)} %copy-done.3, s32[32]{0:T(128)S(1)} %copy-done.2, s32[1]{0:T(128)S(6)} %copy.9.live_ref, bf16[32,256,256]{2,1,0:T(8,128)(2,1)} %tiles_ref.5, bf16[16,256,128]{2,1,0:T(8,128)(2,1)S(1)} %pad_maximum_fusion.near_ref, ...), custom_call_target="tpu_custom_call" | custom-call | tf_op jit(solution)/shard_map/product_one/pallas_call | solution.py:333
  76.6 0.0 copy-start
  76.6 24.3 %all_to_all.30.arrived_ref = bf16[16,272,128]{2,1,0:T(8,128)(2,1)S(1)} all-to-all(bf16[16,272,128]{2,1,0:T(8,128)(2,1)S(1)} %product_one.1), channel_id=1, replica_groups=mesh['quad'=4,'spot'=4,'core'=2,'x'=4,'y'=4] {'x','y'}, dimensions={0} | all-to-all | bytes 2228224 | tf_op jit(solution)/shard_map/reduce_one/all_to_all | solution.py:349
  100.9 0.5 middle.1
  101.4 17.0 %all-gather.2 = bf16[1024,128]{1,0:T(8,128)(2,1)S(1)} all-gather(bf16[256,128]{1,0:T(8,128)(2,1)S(1)} %get-tuple-element.16), channel_id=4, replica_groups=mesh['quad'=4,'spot'=4,'core'=2,'x'=4,'y'=4] {'quad'}, dimensions={0}, use_global_device_ids=true | all-gather | bytes 327680 | tf_op jit(solution)/shard_map/gather_two/all_gather | solution.py:321
  118.4 1.9 collective-permute-start.3
  120.3 1.9 collective-permute-start.2
  122.3 4.6 %collective-permute-start.1 = (bf16[4,256,128]{2,1,0:T(8,128)(2,1)S(1)}, bf16[4,256,128]{2,1,0:T(8,128)(2,1)S(1)}, u32[]{:S(2)}, u32[]{:S(2)}) collective-permute-start(bf16[4,256,128]{2,1,0:T(8,128)(2,1)S(1)} %bitcast.12), channel_id=1, source_target_pairs={{32,0},{48,16},{64,32},{80,48},{96,64},{112,80},{128,96},{144,112}... | collective-permute-start | bytes 786440 | tf_op jit(solution)/shard_map/gather_two/ppermute | solution.py:323
  126.9 7.0 %collective-permute-done.2 = bf16[4,256,128]{2,1,0:T(8,128)(2,1)S(1)} collective-permute-done((bf16[4,256,128]{2,1,0:T(8,128)(2,1)S(1)}, bf16[4,256,128]{2,1,0:T(8,128)(2,1)S(1)}, u32[]{:S(2)}, u32[]{:S(2)}) %collective-permute-start.2) | collective-permute-done | bytes 262176 | tf_op jit(solution)/shard_map/gather_two/ppermute | solution.py:322
  133.8 0.0 collective-permute-done.1
  133.8 0.1 pad_maximum_fusion.1.near_ref
  134.0 8.8 %collective-permute-start.4 = (bf16[16,256,128]{2,1,0:T(8,128)(2,1)S(1)}, bf16[16,256,128]{2,1,0:T(8,128)(2,1)S(1)}, u32[]{:S(2)}, u32[]{:S(2)}) collective-permute-start(bf16[16,256,128]{2,1,0:T(8,128)(2,1)S(1)} %pad_maximum_fusion.1.near_ref), channel_id=1, source_target_pairs={{0,16},{16,0},{1,17},{17,1},{2,18},{18,2},{3,19},{19,3},{4,20},{20... | collective-permute-start | bytes 3145736 | tf_op jit(solution)/shard_map/gather_two/ppermute | solution.py:326
  142.8 2.3 %collective-permute-done.4.far_ref = bf16[16,256,128]{2,1,0:T(8,128)(2,1)S(1)} collective-permute-done((bf16[16,256,128]{2,1,0:T(8,128)(2,1)S(1)}, bf16[16,256,128]{2,1,0:T(8,128)(2,1)S(1)}, u32[]{:S(2)}, u32[]{:S(2)}) %collective-permute-start.4) | collective-permute-done | bytes 1048608 | tf_op jit(solution)/shard_map/gather_two/ppermute | solution.py:326
  145.0 2.0 product_two.1
  147.0 19.2 %all_to_all.31.arrived_ref = bf16[16,256,128]{2,1,0:T(8,128)(2,1)S(1)} all-to-all(bf16[16,256,128]{2,1,0:T(8,128)(2,1)S(1)} %product_two.1), channel_id=1, replica_groups=mesh['quad'=4,'spot'=4,'core'=2,'x'=4,'y'=4] {'x','y'}, dimensions={0} | all-to-all | bytes 2097152 | tf_op jit(solution)/shard_map/reduce_two/all_to_all | solution.py:363
  166.3 0.5 last.1
  166.7 12.9 %all_to_all.32 = f32[32,8,128]{2,1,0:T(8,128)S(1)} all-to-all(f32[32,8,128]{2,1,0:T(8,128)S(1)} %get-tuple-element.19), channel_id=1, replica_groups=mesh['quad'=4,'spot'=4,'core'=2,'x'=4,'y'=4] {'core','x','y'}, dimensions={0} | all-to-all | bytes 262144 | tf_op jit(solution)/shard_map/gram/all_to_all | solution.py:374
  179.7 17.8 %all_to_all.33 = f32[16,8,128]{2,1,0:T(8,128)S(1)} all-to-all(f32[16,8,128]{2,1,0:T(8,128)S(1)} %broadcast_in_dim.7), channel_id=1, replica_groups=mesh['quad'=4,'spot'=4,'core'=2,'x'=4,'y'=4] {'quad','spot'}, dimensions={0} | all-to-all | bytes 131072 | tf_op jit(solution)/shard_map/gram/all_to_all | solution.py:376
  197.6 13.0 %all_to_all.34.grams_ref = f32[32,8,128]{2,1,0:T(8,128)S(1)} all-to-all(f32[32,8,128]{2,1,0:T(8,128)S(1)} %broadcast_in_dim.8), channel_id=1, replica_groups=mesh['quad'=4,'spot'=4,'core'=2,'x'=4,'y'=4] {'core','x','y'}, dimensions={0} | all-to-all | bytes 262144 | tf_op jit(solution)/shard_map/gram/all_to_all | solution.py:378
  210.6 11.0 %finish.1 = f32[256,128]{1,0:T(8,128)} custom-call(f32[32,8,128]{2,1,0:T(8,128)S(1)} %all_to_all.34.grams_ref, f32[256,128]{1,0:T(8,128)S(1)} %get-tuple-element.20.fresh_ref), custom_call_target="tpu_custom_call" | custom-call | tf_op jit(solution)/shard_map/finish/pallas_call | solution.py:380
  (12 shorter events, 0.1 us)
Async XLA Ops:
  0.7 34.9 %copy-start.1 = (bf16[256,128]{1,0:T(8,128)(2,1)S(1)}, bf16[256,128]{1,0:T(8,128)(2,1)}, u32[]{:S(2)}) copy-start(bf16[256,128]{1,0:T(8,128)(2,1)} %initial_ref.3) | copy-start | bytes 196612
  4.5 68.1 %copy-start.2 = (s32[32]{0:T(128)S(1)}, s32[32]{0:T(128)}, u32[]{:S(2)}) copy-start(s32[32]{0:T(128)} %cols_ref.5) | copy-start | bytes 388
  4.5 68.1 %copy-start.3 = (s32[32]{0:T(128)S(1)}, s32[32]{0:T(128)}, u32[]{:S(2)}) copy-start(s32[32]{0:T(128)} %rows_ref.3) | copy-start | bytes 388
  4.6 27.3 %all-to-all-start = ((f32[16,8,128]{2,1,0:T(8,128)}), f32[16,8,128]{2,1,0:T(8,128)S(1)}, u32[]{:S(2)}, u32[]{:S(2)}) async-start(f32[16,8,128]{2,1,0:T(8,128)} %col_degree.1), calls=%async_computation | async-start | bytes 131072 | tf_op jit(solution)/shard_map/col_degree/all_to_all | solution.py:298
  68.1 4.6 %collective-permute-start = (bf16[16,256,128]{2,1,0:T(8,128)(2,1)S(1)}, bf16[16,256,128]{2,1,0:T(8,128)(2,1)S(1)}, u32[]{:S(2)}, u32[]{:S(2)}) collective-permute-start(bf16[16,256,128]{2,1,0:T(8,128)(2,1)S(1)} %pad_maximum_fusion.near_ref), channel_id=1, source_target_pairs={{0,16},{16,0},{1,17},{17,1},{2,18},{18,2},{3,19},{19,3},{4,20},{20... | collective-permute-start | bytes 3145736 | tf_op jit(solution)/shard_map/gather_one/ppermute | solution.py:345
  76.6 68.4 %copy-start = (bf16[32,256,256]{2,1,0:T(8,128)(2,1)S(1)}, bf16[32,256,256]{2,1,0:T(8,128)(2,1)}, u32[]{:S(2)}) copy-start(bf16[32,256,256]{2,1,0:T(8,128)(2,1)} %tiles_ref.5) | copy-start | bytes 12582916
  118.4 8.4 %collective-permute-start.3 = (bf16[4,256,128]{2,1,0:T(8,128)(2,1)S(1)}, bf16[4,256,128]{2,1,0:T(8,128)(2,1)S(1)}, u32[]{:S(2)}, u32[]{:S(2)}) collective-permute-start(bf16[4,256,128]{2,1,0:T(8,128)(2,1)S(1)} %bitcast.10), channel_id=1, source_target_pairs={{480,0},{496,16},{0,32},{16,48},{32,64},{48,80},{64,96},{80,112},{... | collective-permute-start | bytes 786440 | tf_op jit(solution)/shard_map/gather_two/ppermute | solution.py:324
  120.3 13.5 %collective-permute-start.2 = (bf16[4,256,128]{2,1,0:T(8,128)(2,1)S(1)}, bf16[4,256,128]{2,1,0:T(8,128)(2,1)S(1)}, u32[]{:S(2)}, u32[]{:S(2)}) collective-permute-start(bf16[4,256,128]{2,1,0:T(8,128)(2,1)S(1)} %bitcast.11), channel_id=1, source_target_pairs={{64,0},{464,16},{96,32},{496,48},{128,64},{16,80},{160,96},{48,112... | collective-permute-start | bytes 786440 | tf_op jit(solution)/shard_map/gather_two/ppermute | solution.py:322
  122.3 11.6 %collective-permute-start.1 = (bf16[4,256,128]{2,1,0:T(8,128)(2,1)S(1)}, bf16[4,256,128]{2,1,0:T(8,128)(2,1)S(1)}, u32[]{:S(2)}, u32[]{:S(2)}) collective-permute-start(bf16[4,256,128]{2,1,0:T(8,128)(2,1)S(1)} %bitcast.12), channel_id=1, source_target_pairs={{32,0},{48,16},{64,32},{80,48},{96,64},{112,80},{128,96},{144,112}... | collective-permute-start | bytes 786440 | tf_op jit(solution)/shard_map/gather_two/ppermute | solution.py:323
  134.0 11.0 %collective-permute-start.4 = (bf16[16,256,128]{2,1,0:T(8,128)(2,1)S(1)}, bf16[16,256,128]{2,1,0:T(8,128)(2,1)S(1)}, u32[]{:S(2)}, u32[]{:S(2)}) collective-permute-start(bf16[16,256,128]{2,1,0:T(8,128)(2,1)S(1)} %pad_maximum_fusion.1.near_ref), channel_id=1, source_target_pairs={{0,16},{16,0},{1,17},{17,1},{2,18},{18,2},{3,19},{19,3},{4,20},{20... | collective-permute-start | bytes 3145736 | tf_op jit(solution)/shard_map/gather_two/ppermute | solution.py:326

commit v6 on v5

--- a/solution.py
+++ b/solution.py
@@ -319,7 +319,7 @@
     def gather(sent):
         chips = levels + ("core",)
         mine = lax.all_gather(sent, "quad", axis=0)
-        two = lax.ppermute(mine, chips, from_level(2, -2))
+        two = lax.ppermute(mine, chips, from_level(-2, 2))
         one = lax.ppermute(mine, chips, from_level(1, 1))
         three = lax.ppermute(mine, chips, from_level(-1, -1))
         near = jnp.concatenate([mine, one, two, three], axis=0)

time: 222 us -> 221 us (level)
    ppermute x1, waiting for transfers between devices: 0.01 us -> 6.3 us  [gather(): one = lax.ppermute(mine, chips, from_level(1, 1))]
    ppermute x1, waiting for transfers between devices: 6.98 us -> 2.58 us  [gather(): two = lax.ppermute(mine, chips, from_level(-2, 2))]
    ppermute x1, starting transfers between devices: 8.77 us -> 5.92 us  [gather(): return (near, lax.ppermute(near, 'core', swap))]
  transfers between devices with their start and end apart: 6 -> 6, of which waited for: 4 -> 5; matrix products, arithmetic and copies ran while one was open for 0% -> 0% of each run, Pallas kernels for 0% -> 0%
where the time goes in v6:
time: 221 us; the launch traced here: 220 us
  blocking collectives  139 us (63%)
  starting transfers between devices  32.9 us (15%)
  waiting for transfers between devices  25.1 us (11%)
  Pallas kernels  22.4 us (10%)
    all_to_all x2, blocking collectives, shards(): arrived = lax.all_to_all(partial_value, ('x', 'y'), 0, 0, tiled=True)  42.9 us
    all_gather x1, blocking collectives, shards(): lax.all_gather(sent[:SIDE - 1], levels + ('core',), axis=0, axis_index_gr...  31.7 us
    all_to_all x1, blocking collectives, shards(): piece = jnp.sum(lax.all_to_all(spread, levels, 0, 0, tiled=True), axis=0)  17.8 us
    all_gather x1, blocking collectives, gather(): mine = lax.all_gather(sent, 'quad', axis=0)  16.6 us
    all_to_all x1, starting transfers between devices, shards(): degrees = lax.all_to_all(part, levels, 0, 0, tiled=True)  16 us
    all_to_all x1, blocking collectives, shards(): grams = lax.all_to_all(spread, plane, 0, 0, tiled=True)  13 us
    all_to_all x1, blocking collectives, shards(): piece = jnp.sum(lax.all_to_all(grams, plane, 0, 0, tiled=True), axis=0)  12.9 us
    all_to_all x1, waiting for transfers between devices, shards(): degrees = lax.all_to_all(part, levels, 0, 0, tiled=True)  11.5 us
  transfers between devices with their start and end apart: 6, of which 5 were waited for; matrix products, arithmetic and copies ran while one was open for 0% of the time, Pallas kernels for 0%

profile of v6, /device:TPU:1, one launch (start us, length us, event | category | flops | bytes accessed | tf_op | source)
XLA Modules:
  0.0 220.3 jit_solution(11193770036122051299)
XLA Ops:
  0.7 3.9 %col_degree.1 = f32[16,8,128]{2,1,0:T(8,128)} custom-call(s32[32]{0:T(128)} %cols_ref.5, s32[1]{0:T(128)S(6)} %copy.9.live_ref, bf16[32,256,256]{2,1,0:T(8,128)(2,1)} %tiles_ref.5, bf16[256,128]{1,0:T(8,128)(2,1)} %initial_ref.3), custom_call_target="tpu_custom_call" | custom-call | tf_op jit(solution)/shard_map/col_degree/pallas_call | solution.py:286
  4.5 0.0 copy-start.2
  4.5 0.0 copy-start.3
  4.6 16.0 %all-to-all-start = ((f32[16,8,128]{2,1,0:T(8,128)}), f32[16,8,128]{2,1,0:T(8,128)S(1)}, u32[]{:S(2)}, u32[]{:S(2)}) async-start(f32[16,8,128]{2,1,0:T(8,128)} %col_degree.1), calls=%async_computation | async-start | bytes 131072 | tf_op jit(solution)/shard_map/col_degree/all_to_all | solution.py:298
  20.6 0.1 pad_add_fusion.place_ref
  20.7 11.5 %all-to-all-done = f32[16,8,128]{2,1,0:T(8,128)S(1)} async-done(((f32[16,8,128]{2,1,0:T(8,128)}), f32[16,8,128]{2,1,0:T(8,128)S(1)}, u32[]{:S(2)}, u32[]{:S(2)}) %all-to-all-start) | async-done | bytes 65568 | tf_op jit(solution)/shard_map/col_degree/all_to_all | solution.py:298
  32.2 3.7 %all-gather = f32[32,8,128]{2,1,0:T(8,128)S(1)} all-gather(f32[16,8,128]{2,1,0:T(8,128)S(1)} %all-to-all-done), channel_id=2, replica_groups=mesh['quad'=4,'spot'=4,'core'=2,'x'=4,'y'=4] {'core'}, dimensions={0}, use_global_device_ids=true | all-gather | bytes 196608 | tf_op jit(solution)/shard_map/col_degree/all_gather | solution.py:299
  35.8 0.7 scale.1
  36.5 31.7 %all-gather.3 = bf16[16,255,128]{2,1,0:T(8,128)(2,1)S(1)} all-gather(bf16[1,255,128]{2,1,0:T(8,128)(2,1)S(1)} %slice_bitcast_fusion), channel_id=3, replica_groups={{0,32,64,96,144,176,208,240,256,288,320,352,400,432,464,496},{16,48,80,..., dimensions={0}, use_global_device_ids=true | all-gather | bytes 1109760 | tf_op jit(solution)/shard_map/gather_one/all_gather | solution.py:343
  68.2 0.1 pad_maximum_fusion.near_ref
  68.3 2.1 collective-permute-start
  70.4 2.5 %collective-permute-done.far_ref = bf16[16,256,128]{2,1,0:T(8,128)(2,1)S(1)} collective-permute-done((bf16[16,256,128]{2,1,0:T(8,128)(2,1)S(1)}, bf16[16,256,128]{2,1,0:T(8,128)(2,1)S(1)}, u32[]{:S(2)}, u32[]{:S(2)}) %collective-permute-start) | collective-permute-done | bytes 1048608 | tf_op jit(solution)/shard_map/gather_one/ppermute | solution.py:345
  72.9 4.0 %product_one.1 = bf16[16,272,128]{2,1,0:T(8,128)(2,1)S(1)} custom-call(s32[3]{0:T(128)S(1)} %pad_add_fusion.place_ref, s32[32]{0:T(128)S(1)} %copy-done.3, s32[32]{0:T(128)S(1)} %copy-done.2, s32[1]{0:T(128)S(6)} %copy.9.live_ref, bf16[32,256,256]{2,1,0:T(8,128)(2,1)} %tiles_ref.5, bf16[16,256,128]{2,1,0:T(8,128)(2,1)S(1)} %pad_maximum_fusion.near_ref, ...), custom_call_target="tpu_custom_call" | custom-call | tf_op jit(solution)/shard_map/product_one/pallas_call | solution.py:333
  76.9 0.0 copy-start
  76.9 24.0 %all_to_all.30.arrived_ref = bf16[16,272,128]{2,1,0:T(8,128)(2,1)S(1)} all-to-all(bf16[16,272,128]{2,1,0:T(8,128)(2,1)S(1)} %product_one.1), channel_id=1, replica_groups=mesh['quad'=4,'spot'=4,'core'=2,'x'=4,'y'=4] {'x','y'}, dimensions={0} | all-to-all | bytes 2228224 | tf_op jit(solution)/shard_map/reduce_one/all_to_all | solution.py:349
  100.9 0.5 middle.1
  101.4 16.6 %all-gather.2 = bf16[1024,128]{1,0:T(8,128)(2,1)S(1)} all-gather(bf16[256,128]{1,0:T(8,128)(2,1)S(1)} %get-tuple-element.16), channel_id=4, replica_groups=mesh['quad'=4,'spot'=4,'core'=2,'x'=4,'y'=4] {'quad'}, dimensions={0}, use_global_device_ids=true | all-gather | bytes 327680 | tf_op jit(solution)/shard_map/gather_two/all_gather | solution.py:321
  118.0 1.9 collective-permute-start.3
  119.9 3.5 %collective-permute-start.2 = (bf16[4,256,128]{2,1,0:T(8,128)(2,1)S(1)}, bf16[4,256,128]{2,1,0:T(8,128)(2,1)S(1)}, u32[]{:S(2)}, u32[]{:S(2)}) collective-permute-start(bf16[4,256,128]{2,1,0:T(8,128)(2,1)S(1)} %bitcast.11), channel_id=1, source_target_pairs={{448,0},{80,16},{480,32},{112,48},{0,64},{144,80},{32,96},{176,112... | collective-permute-start | bytes 786440 | tf_op jit(solution)/shard_map/gather_two/ppermute | solution.py:322
  123.4 3.4 %collective-permute-start.1 = (bf16[4,256,128]{2,1,0:T(8,128)(2,1)S(1)}, bf16[4,256,128]{2,1,0:T(8,128)(2,1)S(1)}, u32[]{:S(2)}, u32[]{:S(2)}) collective-permute-start(bf16[4,256,128]{2,1,0:T(8,128)(2,1)S(1)} %bitcast.12), channel_id=1, source_target_pairs={{32,0},{48,16},{64,32},{80,48},{96,64},{112,80},{128,96},{144,112}... | collective-permute-start | bytes 786440 | tf_op jit(solution)/shard_map/gather_two/ppermute | solution.py:323
  126.9 2.6 %collective-permute-done.2 = bf16[4,256,128]{2,1,0:T(8,128)(2,1)S(1)} collective-permute-done((bf16[4,256,128]{2,1,0:T(8,128)(2,1)S(1)}, bf16[4,256,128]{2,1,0:T(8,128)(2,1)S(1)}, u32[]{:S(2)}, u32[]{:S(2)}) %collective-permute-start.2) | collective-permute-done | bytes 262176 | tf_op jit(solution)/shard_map/gather_two/ppermute | solution.py:322
  129.5 6.3 %collective-permute-done.1 = bf16[4,256,128]{2,1,0:T(8,128)(2,1)S(1)} collective-permute-done((bf16[4,256,128]{2,1,0:T(8,128)(2,1)S(1)}, bf16[4,256,128]{2,1,0:T(8,128)(2,1)S(1)}, u32[]{:S(2)}, u32[]{:S(2)}) %collective-permute-start.1) | collective-permute-done | bytes 262176 | tf_op jit(solution)/shard_map/gather_two/ppermute | solution.py:323
  135.8 0.1 pad_maximum_fusion.1.near_ref
  135.9 5.9 %collective-permute-start.4 = (bf16[16,256,128]{2,1,0:T(8,128)(2,1)S(1)}, bf16[16,256,128]{2,1,0:T(8,128)(2,1)S(1)}, u32[]{:S(2)}, u32[]{:S(2)}) collective-permute-start(bf16[16,256,128]{2,1,0:T(8,128)(2,1)S(1)} %pad_maximum_fusion.1.near_ref), channel_id=1, source_target_pairs={{0,16},{16,0},{1,17},{17,1},{2,18},{18,2},{3,19},{19,3},{4,20},{20... | collective-permute-start | bytes 3145736 | tf_op jit(solution)/shard_map/gather_two/ppermute | solution.py:326
  141.8 2.3 %collective-permute-done.4.far_ref = bf16[16,256,128]{2,1,0:T(8,128)(2,1)S(1)} collective-permute-done((bf16[16,256,128]{2,1,0:T(8,128)(2,1)S(1)}, bf16[16,256,128]{2,1,0:T(8,128)(2,1)S(1)}, u32[]{:S(2)}, u32[]{:S(2)}) %collective-permute-start.4) | collective-permute-done | bytes 1048608 | tf_op jit(solution)/shard_map/gather_two/ppermute | solution.py:326
  144.1 2.0 product_two.1
  146.1 18.9 %all_to_all.31.arrived_ref = bf16[16,256,128]{2,1,0:T(8,128)(2,1)S(1)} all-to-all(bf16[16,256,128]{2,1,0:T(8,128)(2,1)S(1)} %product_two.1), channel_id=1, replica_groups=mesh['quad'=4,'spot'=4,'core'=2,'x'=4,'y'=4] {'x','y'}, dimensions={0} | all-to-all | bytes 2097152 | tf_op jit(solution)/shard_map/reduce_two/all_to_all | solution.py:363
  165.0 0.5 last.1
  165.4 12.9 %all_to_all.32 = f32[32,8,128]{2,1,0:T(8,128)S(1)} all-to-all(f32[32,8,128]{2,1,0:T(8,128)S(1)} %get-tuple-element.19), channel_id=1, replica_groups=mesh['quad'=4,'spot'=4,'core'=2,'x'=4,'y'=4] {'core','x','y'}, dimensions={0} | all-to-all | bytes 262144 | tf_op jit(solution)/shard_map/gram/all_to_all | solution.py:374
  178.4 17.8 %all_to_all.33 = f32[16,8,128]{2,1,0:T(8,128)S(1)} all-to-all(f32[16,8,128]{2,1,0:T(8,128)S(1)} %broadcast_in_dim.7), channel_id=1, replica_groups=mesh['quad'=4,'spot'=4,'core'=2,'x'=4,'y'=4] {'quad','spot'}, dimensions={0} | all-to-all | bytes 131072 | tf_op jit(solution)/shard_map/gram/all_to_all | solution.py:376
  196.3 13.0 %all_to_all.34.grams_ref = f32[32,8,128]{2,1,0:T(8,128)S(1)} all-to-all(f32[32,8,128]{2,1,0:T(8,128)S(1)} %broadcast_in_dim.8), channel_id=1, replica_groups=mesh['quad'=4,'spot'=4,'core'=2,'x'=4,'y'=4] {'core','x','y'}, dimensions={0} | all-to-all | bytes 262144 | tf_op jit(solution)/shard_map/gram/all_to_all | solution.py:378
  209.3 11.0 %finish.1 = f32[256,128]{1,0:T(8,128)} custom-call(f32[32,8,128]{2,1,0:T(8,128)S(1)} %all_to_all.34.grams_ref, f32[256,128]{1,0:T(8,128)S(1)} %get-tuple-element.20.fresh_ref), custom_call_target="tpu_custom_call" | custom-call | tf_op jit(solution)/shard_map/finish/pallas_call | solution.py:380
  (12 shorter events, 0.1 us)
Async XLA Ops:
  0.7 35.2 %copy-start.1 = (bf16[256,128]{1,0:T(8,128)(2,1)S(1)}, bf16[256,128]{1,0:T(8,128)(2,1)}, u32[]{:S(2)}) copy-start(bf16[256,128]{1,0:T(8,128)(2,1)} %initial_ref.3) | copy-start | bytes 196612
  4.5 68.4 %copy-start.2 = (s32[32]{0:T(128)S(1)}, s32[32]{0:T(128)}, u32[]{:S(2)}) copy-start(s32[32]{0:T(128)} %cols_ref.5) | copy-start | bytes 388
  4.5 68.4 %copy-start.3 = (s32[32]{0:T(128)S(1)}, s32[32]{0:T(128)}, u32[]{:S(2)}) copy-start(s32[32]{0:T(128)} %rows_ref.3) | copy-start | bytes 388
  4.6 27.6 %all-to-all-start = ((f32[16,8,128]{2,1,0:T(8,128)}), f32[16,8,128]{2,1,0:T(8,128)S(1)}, u32[]{:S(2)}, u32[]{:S(2)}) async-start(f32[16,8,128]{2,1,0:T(8,128)} %col_degree.1), calls=%async_computation | async-start | bytes 131072 | tf_op jit(solution)/shard_map/col_degree/all_to_all | solution.py:298
  68.3 4.6 %collective-permute-start = (bf16[16,256,128]{2,1,0:T(8,128)(2,1)S(1)}, bf16[16,256,128]{2,1,0:T(8,128)(2,1)S(1)}, u32[]{:S(2)}, u32[]{:S(2)}) collective-permute-start(bf16[16,256,128]{2,1,0:T(8,128)(2,1)S(1)} %pad_maximum_fusion.near_ref), channel_id=1, source_target_pairs={{0,16},{16,0},{1,17},{17,1},{2,18},{18,2},{3,19},{19,3},{4,20},{20... | collective-permute-start | bytes 3145736 | tf_op jit(solution)/shard_map/gather_one/ppermute | solution.py:345
  76.9 67.2 %copy-start = (bf16[32,256,256]{2,1,0:T(8,128)(2,1)S(1)}, bf16[32,256,256]{2,1,0:T(8,128)(2,1)}, u32[]{:S(2)}) copy-start(bf16[32,256,256]{2,1,0:T(8,128)(2,1)} %tiles_ref.5) | copy-start | bytes 12582916
  118.0 8.9 %collective-permute-start.3 = (bf16[4,256,128]{2,1,0:T(8,128)(2,1)S(1)}, bf16[4,256,128]{2,1,0:T(8,128)(2,1)S(1)}, u32[]{:S(2)}, u32[]{:S(2)}) collective-permute-start(bf16[4,256,128]{2,1,0:T(8,128)(2,1)S(1)} %bitcast.10), channel_id=1, source_target_pairs={{480,0},{496,16},{0,32},{16,48},{32,64},{48,80},{64,96},{80,112},{... | collective-permute-start | bytes 786440 | tf_op jit(solution)/shard_map/gather_two/ppermute | solution.py:324
  119.9 9.6 %collective-permute-start.2 = (bf16[4,256,128]{2,1,0:T(8,128)(2,1)S(1)}, bf16[4,256,128]{2,1,0:T(8,128)(2,1)S(1)}, u32[]{:S(2)}, u32[]{:S(2)}) collective-permute-start(bf16[4,256,128]{2,1,0:T(8,128)(2,1)S(1)} %bitcast.11), channel_id=1, source_target_pairs={{448,0},{80,16},{480,32},{112,48},{0,64},{144,80},{32,96},{176,112... | collective-permute-start | bytes 786440 | tf_op jit(solution)/shard_map/gather_two/ppermute | solution.py:322
  123.4 12.3 %collective-permute-start.1 = (bf16[4,256,128]{2,1,0:T(8,128)(2,1)S(1)}, bf16[4,256,128]{2,1,0:T(8,128)(2,1)S(1)}, u32[]{:S(2)}, u32[]{:S(2)}) collective-permute-start(bf16[4,256,128]{2,1,0:T(8,128)(2,1)S(1)} %bitcast.12), channel_id=1, source_target_pairs={{32,0},{48,16},{64,32},{80,48},{96,64},{112,80},{128,96},{144,112}... | collective-permute-start | bytes 786440 | tf_op jit(solution)/shard_map/gather_two/ppermute | solution.py:323
  135.9 8.2 %collective-permute-start.4 = (bf16[16,256,128]{2,1,0:T(8,128)(2,1)S(1)}, bf16[16,256,128]{2,1,0:T(8,128)(2,1)S(1)}, u32[]{:S(2)}, u32[]{:S(2)}) collective-permute-start(bf16[16,256,128]{2,1,0:T(8,128)(2,1)S(1)} %pad_maximum_fusion.1.near_ref), channel_id=1, source_target_pairs={{0,16},{16,0},{1,17},{17,1},{2,18},{18,2},{3,19},{19,3},{4,20},{20... | collective-permute-start | bytes 3145736 | tf_op jit(solution)/shard_map/gather_two/ppermute | solution.py:326

commit v7 on v6

--- a/solution.py
+++ b/solution.py
@@ -319,9 +319,9 @@
     def gather(sent):
         chips = levels + ("core",)
         mine = lax.all_gather(sent, "quad", axis=0)
-        two = lax.ppermute(mine, chips, from_level(-2, 2))
         one = lax.ppermute(mine, chips, from_level(1, 1))
         three = lax.ppermute(mine, chips, from_level(-1, -1))
+        two = lax.ppermute(mine, chips, from_level(-2, 2))
         near = jnp.concatenate([mine, one, two, three], axis=0)
         return near, lax.ppermute(near, "core", swap)
 

time: 221 us -> 220 us (level)
  starting transfers between devices: 32.9 us -> 29.4 us
    ppermute x1, starting transfers between devices: 5.92 us -> 3.16 us  [gather(): return (near, lax.ppermute(near, 'core', swap))]
where the time goes in v7:
time: 220 us; the launch traced here: 219 us
  blocking collectives  139 us (63%)
  starting transfers between devices  29.4 us (13%)
  waiting for transfers between devices  26.9 us (12%)
  Pallas kernels  22.4 us (10%)
    all_to_all x2, blocking collectives, shards(): arrived = lax.all_to_all(partial_value, ('x', 'y'), 0, 0, tiled=True)  43.4 us
    all_gather x1, blocking collectives, shards(): lax.all_gather(sent[:SIDE - 1], levels + ('core',), axis=0, axis_index_gr...  31.7 us
    all_to_all x1, blocking collectives, shards(): piece = jnp.sum(lax.all_to_all(spread, levels, 0, 0, tiled=True), axis=0)  17.9 us
    all_gather x1, blocking collectives, gather(): mine = lax.all_gather(sent, 'quad', axis=0)  16.8 us
    all_to_all x1, starting transfers between devices, shards(): degrees = lax.all_to_all(part, levels, 0, 0, tiled=True)  15.8 us
    all_to_all x1, blocking collectives, shards(): grams = lax.all_to_all(spread, plane, 0, 0, tiled=True)  13 us
    all_to_all x1, blocking collectives, shards(): piece = jnp.sum(lax.all_to_all(grams, plane, 0, 0, tiled=True), axis=0)  12.9 us
    all_to_all x1, waiting for transfers between devices, shards(): degrees = lax.all_to_all(part, levels, 0, 0, tiled=True)  11.5 us
  transfers between devices with their start and end apart: 6, of which 5 were waited for; matrix products, arithmetic and copies ran while one was open for 0% of the time, Pallas kernels for 0%

profile of v7, /device:TPU:1, one launch (start us, length us, event | category | flops | bytes accessed | tf_op | source)
XLA Modules:
  0.0 219.3 jit_solution(11193770036122051299)
XLA Ops:
  0.7 3.9 %col_degree.1 = f32[16,8,128]{2,1,0:T(8,128)} custom-call(s32[32]{0:T(128)} %cols_ref.5, s32[1]{0:T(128)S(6)} %copy.9.live_ref, bf16[32,256,256]{2,1,0:T(8,128)(2,1)} %tiles_ref.5, bf16[256,128]{1,0:T(8,128)(2,1)} %initial_ref.3), custom_call_target="tpu_custom_call" | custom-call | tf_op jit(solution)/shard_map/col_degree/pallas_call | solution.py:286
  4.5 0.0 copy-start.2
  4.5 0.0 copy-start.3
  4.6 15.8 %all-to-all-start = ((f32[16,8,128]{2,1,0:T(8,128)}), f32[16,8,128]{2,1,0:T(8,128)S(1)}, u32[]{:S(2)}, u32[]{:S(2)}) async-start(f32[16,8,128]{2,1,0:T(8,128)} %col_degree.1), calls=%async_computation | async-start | bytes 131072 | tf_op jit(solution)/shard_map/col_degree/all_to_all | solution.py:298
  20.3 0.1 pad_add_fusion.place_ref
  20.4 11.5 %all-to-all-done = f32[16,8,128]{2,1,0:T(8,128)S(1)} async-done(((f32[16,8,128]{2,1,0:T(8,128)}), f32[16,8,128]{2,1,0:T(8,128)S(1)}, u32[]{:S(2)}, u32[]{:S(2)}) %all-to-all-start) | async-done | bytes 65568 | tf_op jit(solution)/shard_map/col_degree/all_to_all | solution.py:298
  31.9 3.6 %all-gather = f32[32,8,128]{2,1,0:T(8,128)S(1)} all-gather(f32[16,8,128]{2,1,0:T(8,128)S(1)} %all-to-all-done), channel_id=2, replica_groups=mesh['quad'=4,'spot'=4,'core'=2,'x'=4,'y'=4] {'core'}, dimensions={0}, use_global_device_ids=true | all-gather | bytes 196608 | tf_op jit(solution)/shard_map/col_degree/all_gather | solution.py:299
  35.5 0.7 scale.1
  36.2 31.7 %all-gather.3 = bf16[16,255,128]{2,1,0:T(8,128)(2,1)S(1)} all-gather(bf16[1,255,128]{2,1,0:T(8,128)(2,1)S(1)} %slice_bitcast_fusion), channel_id=3, replica_groups={{0,32,64,96,144,176,208,240,256,288,320,352,400,432,464,496},{16,48,80,..., dimensions={0}, use_global_device_ids=true | all-gather | bytes 1109760 | tf_op jit(solution)/shard_map/gather_one/all_gather | solution.py:343
  67.9 0.1 pad_maximum_fusion.near_ref
  68.1 2.1 collective-permute-start
  70.1 2.5 %collective-permute-done.far_ref = bf16[16,256,128]{2,1,0:T(8,128)(2,1)S(1)} collective-permute-done((bf16[16,256,128]{2,1,0:T(8,128)(2,1)S(1)}, bf16[16,256,128]{2,1,0:T(8,128)(2,1)S(1)}, u32[]{:S(2)}, u32[]{:S(2)}) %collective-permute-start) | collective-permute-done | bytes 1048608 | tf_op jit(solution)/shard_map/gather_one/ppermute | solution.py:345
  72.6 4.0 %product_one.1 = bf16[16,272,128]{2,1,0:T(8,128)(2,1)S(1)} custom-call(s32[3]{0:T(128)S(1)} %pad_add_fusion.place_ref, s32[32]{0:T(128)S(1)} %copy-done.3, s32[32]{0:T(128)S(1)} %copy-done.2, s32[1]{0:T(128)S(6)} %copy.9.live_ref, bf16[32,256,256]{2,1,0:T(8,128)(2,1)} %tiles_ref.5, bf16[16,256,128]{2,1,0:T(8,128)(2,1)S(1)} %pad_maximum_fusion.near_ref, ...), custom_call_target="tpu_custom_call" | custom-call | tf_op jit(solution)/shard_map/product_one/pallas_call | solution.py:333
  76.6 0.0 copy-start
  76.6 24.1 %all_to_all.30.arrived_ref = bf16[16,272,128]{2,1,0:T(8,128)(2,1)S(1)} all-to-all(bf16[16,272,128]{2,1,0:T(8,128)(2,1)S(1)} %product_one.1), channel_id=1, replica_groups=mesh['quad'=4,'spot'=4,'core'=2,'x'=4,'y'=4] {'x','y'}, dimensions={0} | all-to-all | bytes 2228224 | tf_op jit(solution)/shard_map/reduce_one/all_to_all | solution.py:349
  100.7 0.5 middle.1
  101.2 16.8 %all-gather.2 = bf16[1024,128]{1,0:T(8,128)(2,1)S(1)} all-gather(bf16[256,128]{1,0:T(8,128)(2,1)S(1)} %get-tuple-element.16), channel_id=4, replica_groups=mesh['quad'=4,'spot'=4,'core'=2,'x'=4,'y'=4] {'quad'}, dimensions={0}, use_global_device_ids=true | all-gather | bytes 327680 | tf_op jit(solution)/shard_map/gather_two/all_gather | solution.py:321
  118.1 1.9 collective-permute-start.3
  120.0 3.2 %collective-permute-start.2 = (bf16[4,256,128]{2,1,0:T(8,128)(2,1)S(1)}, bf16[4,256,128]{2,1,0:T(8,128)(2,1)S(1)}, u32[]{:S(2)}, u32[]{:S(2)}) collective-permute-start(bf16[4,256,128]{2,1,0:T(8,128)(2,1)S(1)} %bitcast.11), channel_id=1, source_target_pairs={{448,0},{80,16},{480,32},{112,48},{0,64},{144,80},{32,96},{176,112... | collective-permute-start | bytes 786440 | tf_op jit(solution)/shard_map/gather_two/ppermute | solution.py:324
  123.2 3.2 %collective-permute-start.1 = (bf16[4,256,128]{2,1,0:T(8,128)(2,1)S(1)}, bf16[4,256,128]{2,1,0:T(8,128)(2,1)S(1)}, u32[]{:S(2)}, u32[]{:S(2)}) collective-permute-start(bf16[4,256,128]{2,1,0:T(8,128)(2,1)S(1)} %bitcast.12), channel_id=1, source_target_pairs={{32,0},{48,16},{64,32},{80,48},{96,64},{112,80},{128,96},{144,112}... | collective-permute-start | bytes 786440 | tf_op jit(solution)/shard_map/gather_two/ppermute | solution.py:322
  126.5 2.6 %collective-permute-done.2 = bf16[4,256,128]{2,1,0:T(8,128)(2,1)S(1)} collective-permute-done((bf16[4,256,128]{2,1,0:T(8,128)(2,1)S(1)}, bf16[4,256,128]{2,1,0:T(8,128)(2,1)S(1)}, u32[]{:S(2)}, u32[]{:S(2)}) %collective-permute-start.2) | collective-permute-done | bytes 262176 | tf_op jit(solution)/shard_map/gather_two/ppermute | solution.py:324
  129.1 8.0 %collective-permute-done.1 = bf16[4,256,128]{2,1,0:T(8,128)(2,1)S(1)} collective-permute-done((bf16[4,256,128]{2,1,0:T(8,128)(2,1)S(1)}, bf16[4,256,128]{2,1,0:T(8,128)(2,1)S(1)}, u32[]{:S(2)}, u32[]{:S(2)}) %collective-permute-start.1) | collective-permute-done | bytes 262176 | tf_op jit(solution)/shard_map/gather_two/ppermute | solution.py:322
  137.2 0.1 pad_maximum_fusion.1.near_ref
  137.3 3.2 %collective-permute-start.4 = (bf16[16,256,128]{2,1,0:T(8,128)(2,1)S(1)}, bf16[16,256,128]{2,1,0:T(8,128)(2,1)S(1)}, u32[]{:S(2)}, u32[]{:S(2)}) collective-permute-start(bf16[16,256,128]{2,1,0:T(8,128)(2,1)S(1)} %pad_maximum_fusion.1.near_ref), channel_id=1, source_target_pairs={{0,16},{16,0},{1,17},{17,1},{2,18},{18,2},{3,19},{19,3},{4,20},{20... | collective-permute-start | bytes 3145736 | tf_op jit(solution)/shard_map/gather_two/ppermute | solution.py:326
  140.5 2.3 %collective-permute-done.4.far_ref = bf16[16,256,128]{2,1,0:T(8,128)(2,1)S(1)} collective-permute-done((bf16[16,256,128]{2,1,0:T(8,128)(2,1)S(1)}, bf16[16,256,128]{2,1,0:T(8,128)(2,1)S(1)}, u32[]{:S(2)}, u32[]{:S(2)}) %collective-permute-start.4) | collective-permute-done | bytes 1048608 | tf_op jit(solution)/shard_map/gather_two/ppermute | solution.py:326
  142.7 2.0 product_two.1
  144.8 19.2 %all_to_all.31.arrived_ref = bf16[16,256,128]{2,1,0:T(8,128)(2,1)S(1)} all-to-all(bf16[16,256,128]{2,1,0:T(8,128)(2,1)S(1)} %product_two.1), channel_id=1, replica_groups=mesh['quad'=4,'spot'=4,'core'=2,'x'=4,'y'=4] {'x','y'}, dimensions={0} | all-to-all | bytes 2097152 | tf_op jit(solution)/shard_map/reduce_two/all_to_all | solution.py:363
  164.0 0.5 last.1
  164.5 12.9 %all_to_all.32 = f32[32,8,128]{2,1,0:T(8,128)S(1)} all-to-all(f32[32,8,128]{2,1,0:T(8,128)S(1)} %get-tuple-element.19), channel_id=1, replica_groups=mesh['quad'=4,'spot'=4,'core'=2,'x'=4,'y'=4] {'core','x','y'}, dimensions={0} | all-to-all | bytes 262144 | tf_op jit(solution)/shard_map/gram/all_to_all | solution.py:374
  177.4 17.9 %all_to_all.33 = f32[16,8,128]{2,1,0:T(8,128)S(1)} all-to-all(f32[16,8,128]{2,1,0:T(8,128)S(1)} %broadcast_in_dim.7), channel_id=1, replica_groups=mesh['quad'=4,'spot'=4,'core'=2,'x'=4,'y'=4] {'quad','spot'}, dimensions={0} | all-to-all | bytes 131072 | tf_op jit(solution)/shard_map/gram/all_to_all | solution.py:376
  195.3 13.0 %all_to_all.34.grams_ref = f32[32,8,128]{2,1,0:T(8,128)S(1)} all-to-all(f32[32,8,128]{2,1,0:T(8,128)S(1)} %broadcast_in_dim.8), channel_id=1, replica_groups=mesh['quad'=4,'spot'=4,'core'=2,'x'=4,'y'=4] {'core','x','y'}, dimensions={0} | all-to-all | bytes 262144 | tf_op jit(solution)/shard_map/gram/all_to_all | solution.py:378
  208.3 11.0 %finish.1 = f32[256,128]{1,0:T(8,128)} custom-call(f32[32,8,128]{2,1,0:T(8,128)S(1)} %all_to_all.34.grams_ref, f32[256,128]{1,0:T(8,128)S(1)} %get-tuple-element.20.fresh_ref), custom_call_target="tpu_custom_call" | custom-call | tf_op jit(solution)/shard_map/finish/pallas_call | solution.py:380
  (12 shorter events, 0.1 us)
Async XLA Ops:
  0.7 34.9 %copy-start.1 = (bf16[256,128]{1,0:T(8,128)(2,1)S(1)}, bf16[256,128]{1,0:T(8,128)(2,1)}, u32[]{:S(2)}) copy-start(bf16[256,128]{1,0:T(8,128)(2,1)} %initial_ref.3) | copy-start | bytes 196612
  4.5 68.1 %copy-start.2 = (s32[32]{0:T(128)S(1)}, s32[32]{0:T(128)}, u32[]{:S(2)}) copy-start(s32[32]{0:T(128)} %cols_ref.5) | copy-start | bytes 388
  4.5 68.1 %copy-start.3 = (s32[32]{0:T(128)S(1)}, s32[32]{0:T(128)}, u32[]{:S(2)}) copy-start(s32[32]{0:T(128)} %rows_ref.3) | copy-start | bytes 388
  4.6 27.3 %all-to-all-start = ((f32[16,8,128]{2,1,0:T(8,128)}), f32[16,8,128]{2,1,0:T(8,128)S(1)}, u32[]{:S(2)}, u32[]{:S(2)}) async-start(f32[16,8,128]{2,1,0:T(8,128)} %col_degree.1), calls=%async_computation | async-start | bytes 131072 | tf_op jit(solution)/shard_map/col_degree/all_to_all | solution.py:298
  68.1 4.6 %collective-permute-start = (bf16[16,256,128]{2,1,0:T(8,128)(2,1)S(1)}, bf16[16,256,128]{2,1,0:T(8,128)(2,1)S(1)}, u32[]{:S(2)}, u32[]{:S(2)}) collective-permute-start(bf16[16,256,128]{2,1,0:T(8,128)(2,1)S(1)} %pad_maximum_fusion.near_ref), channel_id=1, source_target_pairs={{0,16},{16,0},{1,17},{17,1},{2,18},{18,2},{3,19},{19,3},{4,20},{20... | collective-permute-start | bytes 3145736 | tf_op jit(solution)/shard_map/gather_one/ppermute | solution.py:345
  76.6 66.1 %copy-start = (bf16[32,256,256]{2,1,0:T(8,128)(2,1)S(1)}, bf16[32,256,256]{2,1,0:T(8,128)(2,1)}, u32[]{:S(2)}) copy-start(bf16[32,256,256]{2,1,0:T(8,128)(2,1)} %tiles_ref.5) | copy-start | bytes 12582916
  118.1 8.4 %collective-permute-start.3 = (bf16[4,256,128]{2,1,0:T(8,128)(2,1)S(1)}, bf16[4,256,128]{2,1,0:T(8,128)(2,1)S(1)}, u32[]{:S(2)}, u32[]{:S(2)}) collective-permute-start(bf16[4,256,128]{2,1,0:T(8,128)(2,1)S(1)} %bitcast.10), channel_id=1, source_target_pairs={{480,0},{496,16},{0,32},{16,48},{32,64},{48,80},{64,96},{80,112},{... | collective-permute-start | bytes 786440 | tf_op jit(solution)/shard_map/gather_two/ppermute | solution.py:323
  120.0 9.2 %collective-permute-start.2 = (bf16[4,256,128]{2,1,0:T(8,128)(2,1)S(1)}, bf16[4,256,128]{2,1,0:T(8,128)(2,1)S(1)}, u32[]{:S(2)}, u32[]{:S(2)}) collective-permute-start(bf16[4,256,128]{2,1,0:T(8,128)(2,1)S(1)} %bitcast.11), channel_id=1, source_target_pairs={{448,0},{80,16},{480,32},{112,48},{0,64},{144,80},{32,96},{176,112... | collective-permute-start | bytes 786440 | tf_op jit(solution)/shard_map/gather_two/ppermute | solution.py:324
  123.2 13.9 %collective-permute-start.1 = (bf16[4,256,128]{2,1,0:T(8,128)(2,1)S(1)}, bf16[4,256,128]{2,1,0:T(8,128)(2,1)S(1)}, u32[]{:S(2)}, u32[]{:S(2)}) collective-permute-start(bf16[4,256,128]{2,1,0:T(8,128)(2,1)S(1)} %bitcast.12), channel_id=1, source_target_pairs={{32,0},{48,16},{64,32},{80,48},{96,64},{112,80},{128,96},{144,112}... | collective-permute-start | bytes 786440 | tf_op jit(solution)/shard_map/gather_two/ppermute | solution.py:322
  137.3 5.4 %collective-permute-start.4 = (bf16[16,256,128]{2,1,0:T(8,128)(2,1)S(1)}, bf16[16,256,128]{2,1,0:T(8,128)(2,1)S(1)}, u32[]{:S(2)}, u32[]{:S(2)}) collective-permute-start(bf16[16,256,128]{2,1,0:T(8,128)(2,1)S(1)} %pad_maximum_fusion.1.near_ref), channel_id=1, source_target_pairs={{0,16},{16,0},{1,17},{17,1},{2,18},{18,2},{3,19},{19,3},{4,20},{20... | collective-permute-start | bytes 3145736 | tf_op jit(solution)/shard_map/gather_two/ppermute | solution.py:326
